TPU v7x, 32 devices: a whole 2x2x4 slice. The times are simulated.
32 devices in a mesh: row: 8 (over z, y), col: 4 (over x, core).
Axes of the slice: x: 2, y: 2, z: 4, core: 2. Of those that a mesh axis runs over, the one named last changes fastest.
Arguments:
- train_x: float32 [8192, 128], P('row'), may hold values from -6 to 6
- test_x: float32 [4096, 128], P('col'), may hold values from -6 to 6
- scales: float32 [128], replicated, may hold values from 3 to 96
- targets: float32 [8192], P('row')
- factor: float32 [8192, 2048], P('row', 'col'), as said below
- inverses: float32 [8192, 1024], P('row'), as said below
Outputs:
- back_solved: float32 [8192, 4096], P('row', 'col')
- explained: float32 [4096], P('col')
- mean: float32 [4096], P('col')
Inputs may be any that keep to these rules, and one draw needn't show every extreme that they name: factor is zero where its block column is not below its block row: entry [i, c] is zero unless c // 1024 < i // 1024. Each diagonal block of inverses is lower triangular with a positive diagonal.
All inputs are finite; a program needn't handle non-finite values.
Results may differ from a plain program's by a relative error of at most 0.0003.
Values sent between devices are 32-bit elements; how exact they have to be, the bound alone decides.
A program may use at most 128 MiB of HBM per device.

v0:
```python
import jax
import jax.numpy as jnp
from jax import lax
from jax.sharding import PartitionSpec as P


def from_root(array, axis, root):
    mine = lax.axis_index(axis) == root
    return lax.psum(jnp.where(mine, array, jnp.zeros_like(array)), axis)


def transposed_product(left, right):
    return lax.dot_general(left, right, (((0,), (0,)), ((), ())), precision=lax.Precision.HIGHEST)


def kernel_rows(rows_x, scaled_test, scales):
    scaled_rows = rows_x / scales
    squared = (
        jnp.sum(scaled_rows * scaled_rows, axis=1)[:, None]
        + jnp.sum(scaled_test * scaled_test, axis=1)[None, :]
        - 2.0 * jnp.dot(scaled_rows, scaled_test.T, precision=lax.Precision.HIGHEST)
    )
    return jnp.exp(-0.5 * squared)


def local(train_x, test_x, scales, targets, factor, inverses):
    highest = lax.Precision.HIGHEST
    block = inverses.shape[0]
    parts = lax.axis_size("row")
    position = lax.axis_index("row")
    scaled_test = test_x / scales
    kernel = kernel_rows(train_x, scaled_test, scales)
    border = lax.all_gather(factor, "col", axis=1, tiled=True)
    panels = border.shape[1] // block
    residue = kernel
    for step in range(panels):
        candidate = jnp.dot(inverses, residue, precision=highest)
        panel = from_root(candidate, "row", step)
        piece = border[:, step * block : (step + 1) * block]
        residue = residue - jnp.dot(piece, panel, precision=highest)
    whitened = jnp.dot(inverses, residue, precision=highest)
    total_rows = block * parts
    square_total = lax.psum(jnp.sum(whitened * whitened, axis=0), "row")
    back_solved = transposed_product(inverses, whitened)
    for step in reversed(range(panels)):
        piece = border[:, step * block : (step + 1) * block]
        later = lax.psum(transposed_product(piece, back_solved), "row")
        candidate = transposed_product(inverses, whitened - later)
        back_solved = jnp.where(position == step, candidate, back_solved)
    weighted = jnp.dot(targets, back_solved, precision=highest)
    mean = lax.psum(weighted, "row")
    explained = square_total / total_rows
    return (back_solved, explained, mean)


def solution(mesh):
    placed = (P("row", None), P("col", None), P(), P("row"), P("row", "col"), P("row", None))
    return jax.shard_map(
        local,
        mesh=mesh,
        in_specs=placed,
        out_specs=(P("row", "col"), P("col"), P("col")),
        check_vma=False,
    )
```

profile of v0, /device:TPU:0, one launch (start us, length us, event | category | flops | bytes accessed | tf_op | source)
XLA Modules:
  0.0 881.5 jit_solution(4560531433250778403)
XLA Ops:
  8.0 0.0 all-reduce.6.cloned.1.call-start
  8.1 1.6 multiply_reduce_fusion.1
  9.7 6.7 fusion.25
  16.4 32.1 %select_bitcast_fusion.2 = f32[1024,1024]{0,1:T(8,128)} fusion(pred[]{:T(512)S(6)} %eq.8, f32[1024,1024]{1,0:T(8,128)} %param.11, f32[1024,1024]{1,0:T(8,128)} %fusion.25, f32[1024]{0:T(1024)S(1)} %get-tuple-element.7, f32[1024]{0:T(1024)S(1)} %get-tuple-element.6), kind=kOutput, calls=%fused_computation.11 | convolution fusion | flops 12890144768 | bytes 12591105 | tf_op jit(solution)/shard_map/dot_general | solution.py:37
  48.5 0.0 all-reduce.6.cloned.1.call-update
  48.5 0.0 all-gather.2.cloned.1.call-start
  48.5 0.5 all-gather.2.cloned.1.call-update
  49.1 0.0 all-reduce.8.cloned.1.call-start
  49.1 158.5 %all-reduce.6.cloned.1.call-done = f32[1024,1024]{0,1:T(8,128)} async-done(((f32[1024,1024]{0,1:T(8,128)}), f32[1024,1024]{0,1:T(8,128)}) %all-reduce.6.cloned.1.call-update) | async-done | bytes 4194320 | tf_op jit(solution)/shard_map/psum | solution.py:9
  207.6 17.5 %bitcast_subtract_fusion.6 = f32[1024,1024]{1,0:T(8,128)S(1)} fusion(f32[1024,1024]{1,0:T(8,128)} %fusion.25, f32[1024]{0:T(1024)S(1)} %get-tuple-element.7, f32[1024]{0:T(1024)S(1)} %get-tuple-element.6, f32[1024,1024]{0,1:T(8,128)} %all-reduce.6.cloned.1.call-done, f32[1024,2048]{1,0:T(8,128)} %all-gather.2.cloned.1.call-done), kind=kOutput, calls=%fused_computation.8 | convolution fusion | flops 12890144768 | bytes 16785408 | tf_op jit(solution)/shard_map/dot_general | solution.py:40
  225.2 2.0 copy-done.6
  227.2 28.6 %select_bitcast_fusion.1 = f32[1024,1024]{0,1:T(8,128)} fusion(pred[]{:T(512)S(6)} %eq.9, f32[1024,1024]{1,0:T(8,128)S(1)} %bitcast_subtract_fusion.6, f32[1024,1024]{1,0:T(8,128)S(1)} %copy-done.3), kind=kOutput, calls=%fused_computation.10 | convolution fusion | flops 12885950464 | bytes 12582913 | tf_op jit(solution)/shard_map/dot_general | solution.py:37
  255.8 0.0 all-reduce.8.cloned.1.call-update
  255.8 0.0 all-reduce.10.cloned.1.call-start
  255.9 155.4 %all-reduce.8.cloned.1.call-done = f32[1024,1024]{0,1:T(8,128)} async-done(((f32[1024,1024]{0,1:T(8,128)}), f32[1024,1024]{0,1:T(8,128)}) %all-reduce.8.cloned.1.call-update) | async-done | bytes 4194320 | tf_op jit(solution)/shard_map/psum | solution.py:9
  411.3 16.8 %fusion.6 = f32[1024,1024]{0,1:T(8,128)S(1)} fusion(f32[1024,1024]{0,1:T(8,128)} %all-reduce.8.cloned.1.call-done, f32[1024,2048]{1,0:T(8,128)} %all-gather.2.cloned.1.call-done), kind=kOutput, calls=%fused_computation.15 | convolution fusion | flops 12884901888 | bytes 12582912 | tf_op jit(solution)/shard_map/dot_general | solution.py:40
  428.1 15.3 %fusion.2 = (f32[1024]{0:T(1024)S(1)}, f32[1024,1024]{0,1:T(8,128)S(1)}) fusion(f32[1024,1024]{1,0:T(8,128)S(1)} %copy-done.4, f32[1024,1024]{1,0:T(8,128)S(1)} %copy-done.7, f32[1024,1024]{0,1:T(8,128)S(1)} %fusion.6), kind=kOutput, calls=%fused_computation.5 | convolution fusion | flops 12888046592 | bytes 16781312 | tf_op jit(solution)/shard_map/dot_general | solution.py:41
  443.5 14.9 %fusion.28 = f32[1024,1024]{1,0:T(8,128)S(1)} fusion(f32[1024,1024]{0,1:T(8,128)S(1)} %get-tuple-element.11, f32[1024,1024]{1,0:T(8,128)S(1)} %copy-done.4), kind=kOutput, calls=%fused_computation.37 | convolution fusion | flops 12884901888 | bytes 12582912 | tf_op jit(solution)/shard_map/dot_general | solution.py:13
  458.4 2.0 copy-done.5
  460.4 15.3 %fusion.16 = f32[1024,1024]{1,0:T(8,128)} fusion(f32[1024,1024]{1,0:T(8,128)S(1)} %fusion.28, f32[1024,2048]{1,0:T(8,128)S(1)} %bitcast.48), kind=kOutput, calls=%fused_computation.23 | convolution fusion | flops 12884901888 | bytes 12582912 | tf_op jit(solution)/shard_map/dot_general | solution.py:13
  475.7 0.0 all-reduce.10.cloned.1.call-update
  475.8 0.0 all-reduce.12.cloned.1.call-start
  475.8 155.4 %all-reduce.10.cloned.1.call-done = f32[1024,1024]{1,0:T(8,128)} async-done(((f32[1024,1024]{1,0:T(8,128)}), f32[1024,1024]{1,0:T(8,128)}) %all-reduce.10.cloned.1.call-update) | async-done | bytes 4194320 | tf_op jit(solution)/shard_map/psum | solution.py:47
  631.2 18.1 %broadcast_select_fusion = f32[1024,1024]{1,0:T(8,128)S(1)} fusion(f32[1024,1024]{1,0:T(8,128)} %copy-done.5, pred[]{:T(512)S(6)} %eq.9, f32[1024,1024]{1,0:T(8,128)} %param.11, f32[1024,1024]{1,0:T(8,128)} %all-reduce.10.cloned.1.call-done, f32[1024,1024]{0,1:T(8,128)} %copy-done.1), kind=kOutput, calls=%fused_computation.28 | convolution fusion | flops 12886999040 | bytes 20971520 | tf_op jit(solution)/shard_map/dot_general | solution.py:13
  649.3 2.0 copy-done.2
  651.3 16.9 %fusion.13 = f32[1024,1024]{1,0:T(8,128)} fusion(f32[1024,1024]{1,0:T(8,128)S(1)} %broadcast_select_fusion, f32[1024,2048]{1,0:T(8,128)} %all-gather.2.cloned.1.call-done), kind=kOutput, calls=%fused_computation.22 | convolution fusion | flops 12884901888 | bytes 12582912 | tf_op jit(solution)/shard_map/dot_general | solution.py:13
  668.2 155.5 %all-reduce.12.cloned.1.call-done = f32[1024,1024]{1,0:T(8,128)} async-done(((f32[1024,1024]{1,0:T(8,128)}), f32[1024,1024]{1,0:T(8,128)}) %all-reduce.12.cloned.1.call-update) | async-done | bytes 4194320 | tf_op jit(solution)/shard_map/psum | solution.py:47
  823.7 18.2 %select_bitcast_fusion = f32[1024,1024]{0,1:T(8,128)} fusion(f32[1024,1024]{1,0:T(8,128)} %copy-done.2, pred[]{:T(512)S(6)} %eq.8, f32[1024,1024]{1,0:T(8,128)} %param.11, f32[1024,1024]{1,0:T(8,128)} %all-reduce.12.cloned.1.call-done, f32[1024,1024]{0,1:T(8,128)} %copy-done.1), kind=kOutput, calls=%fused_computation.9 | convolution fusion | flops 12886999040 | bytes 20971520 | tf_op jit(solution)/shard_map/dot_general | solution.py:13
  841.8 5.6 copy.10
  847.5 5.8 fusion.29
  853.2 20.3 %all-reduce = (f32[1024]{0:T(1024)S(1)}, f32[1024]{0:T(1024)}) all-reduce(f32[1024]{0:T(1024)S(1)} %get-tuple-element.10, f32[1024]{0:T(1024)S(1)} %bitcast.46), channel_id=1, replica_groups=mesh['row'=8,'col'=4] {'row'}, use_global_device_ids=true, to_apply=%region_7.8 | all-reduce | flops 2048 | bytes 16384 | tf_op jit(solution)/shard_map/psum | solution.py:43
  873.5 0.6 broadcast_multiply_fusion
  (20 shorter events, 0.1 us)
Async XLA Ops:
  8.0 839.5 %copy-start = (f32[1024]{0:T(1024)S(1)}, f32[1024]{0:T(1024)}, u32[]{:S(2)}) copy-start(f32[1024]{0:T(1024)} %param.9) | copy-start | bytes 12292
  8.0 199.6 %all-reduce.6.cloned.1.call-start = ((), (), s32[]{:S(2)}) async-start(), calls=%async_computation | async-start | bytes 8388608 | tf_op jit(solution)/shard_map/psum | solution.py:9
  48.5 159.1 %all-gather.2.cloned.1.call-start = ((), (), s32[]{:S(2)}) async-start(), calls=%async_computation.1 | async-start | bytes 10485760 | tf_op jit(solution)/shard_map/all_gather | solution.py:33
  49.1 362.2 %all-reduce.8.cloned.1.call-start = ((), (), s32[]{:S(2)}) async-start(), calls=%async_computation.2 | async-start | bytes 8388608 | tf_op jit(solution)/shard_map/psum | solution.py:9
  207.6 19.6 %copy-start.3 = (f32[1024,1024]{1,0:T(8,128)S(1)}, f32[1024,1024]{1,0:T(8,128)}, u32[]{:S(2)}) copy-start(f32[1024,1024]{1,0:T(8,128)} %param.11) | copy-start | bytes 12582916
  225.2 2.0 copy-start.6
  255.8 375.4 %all-reduce.10.cloned.1.call-start = ((), (), s32[]{:S(2)}) async-start(), calls=%async_computation.3 | async-start | bytes 8388608 | tf_op jit(solution)/shard_map/psum | solution.py:47
  411.3 16.8 %copy-start.4 = (f32[1024,1024]{1,0:T(8,128)S(1)}, f32[1024,1024]{1,0:T(8,128)}, u32[]{:S(2)}) copy-start(f32[1024,1024]{1,0:T(8,128)} %param.11) | copy-start | bytes 12582916
  411.3 16.8 %copy-start.7 = (f32[1024,1024]{1,0:T(8,128)S(1)}, f32[1024,1024]{1,0:T(8,128)}, u32[]{:S(2)}) copy-start(f32[1024,1024]{1,0:T(8,128)} %copy-done.6) | copy-start | bytes 12582916
  411.3 49.1 %slice-start = ((s8[8388608]{0:T(1024)(128)(4,1)}), s8[4194304]{0:T(1024)(128)(4,1)S(1)}, s32[]{:S(2)}) async-start(s8[8388608]{0:T(1024)(128)(4,1)} %bitcast.47), calls=%async_computation.5 | async-start | bytes 8388608
  428.1 32.3 %slice-start.1 = ((s8[8388608]{0:T(1024)(128)(4,1)}), s8[4194304]{0:T(1024)(128)(4,1)S(1)}, s32[]{:S(2)}) async-start(s8[8388608]{0:T(1024)(128)(4,1)} %bitcast.47), calls=%async_computation.6 | async-start | bytes 8388608
  443.5 14.9 %copy-start.1 = (f32[1024,1024]{0,1:T(8,128)}, f32[1024,1024]{0,1:T(8,128)S(1)}, u32[]{:S(2)}) copy-start(f32[1024,1024]{0,1:T(8,128)S(1)} %get-tuple-element.11) | copy-start | bytes 12582916
  458.4 2.0 copy-start.5
  475.8 347.9 %all-reduce.12.cloned.1.call-start = ((), (), s32[]{:S(2)}) async-start(), calls=%async_computation.4 | async-start | bytes 8388608 | tf_op jit(solution)/shard_map/psum | solution.py:47
  649.3 2.0 copy-start.2
Sparse Core Ops, SparseCore 0:
  48.6 158.9 all-reduce.5
  256.0 155.2 all-reduce.7
  475.9 155.2 all-reduce.9
  668.3 155.2 all-reduce.11
Sparse Core Ops, SparseCore 1:
  50.5 60.8 all-gather.1
where the time goes:
time: 885 us; the launch traced here: 882 us
  waiting for transfers between devices  625 us (71%)
  matrix products  206 us (23%)
  blocking collectives  20.3 us (2%)
  between operations  15.7 us (2%)
  local copies, waits for them, and re-layouts  11.7 us (1%)
    psum x2, waiting for transfers between devices, from_root(): return lax.psum(jnp.where(mine, array, jnp.zeros_like(array)), axis)  314 us
    psum x2, waiting for transfers between devices, local(): later = lax.psum(transposed_product(piece, back_solved), 'row')  311 us
    dot_general x5, matrix products, transposed_product(): lax.dot_general(left, right, (((0,), (0,)), ((), ())), precision=lax.Prec...  83.3 us
    dot_general x2, matrix products, local(): candidate = jnp.dot(inverses, residue, precision=highest)  60.7 us
    dot_general x2, matrix products, local(): residue = residue - jnp.dot(piece, panel, precision=highest)  34.3 us
    psum x1, blocking collectives, local(): square_total = lax.psum(jnp.sum(whitened * whitened, axis=0), 'row')  20.3 us
  transfers between devices with their start and end apart: 5, of which 4 were waited for; matrix products, arithmetic and copies ran while one was open for 0% of the time, Pallas kernels for 0%

commit v1 on v0

v1 whole, which is shorter than its diff:
```python
import jax
import jax.numpy as jnp
from jax import lax
from jax.sharding import PartitionSpec as P

CHUNKS = 4


def product(left, right):
    return jnp.dot(left, right, precision=lax.Precision.HIGH)


def transposed_product(left, right):
    return lax.dot_general(left, right, (((0,), (0,)), ((), ())), precision=lax.Precision.HIGH)


def kernel_rows(rows_x, scaled_test, scales):
    scaled_rows = rows_x / scales
    squared = (
        jnp.sum(scaled_rows * scaled_rows, axis=1)[:, None]
        + jnp.sum(scaled_test * scaled_test, axis=1)[None, :]
        - 2.0 * jnp.dot(scaled_rows, scaled_test.T, precision=lax.Precision.HIGHEST)
    )
    return jnp.exp(-0.5 * squared)


def local(train_x, test_x, scales, targets, factor, inverses):
    block = inverses.shape[0]
    parts = lax.axis_size("row")
    pairs = parts // 2
    position = lax.axis_index("row")
    even = position % 2 == 0
    head = position < 2
    swap = [(r, r ^ 1) for r in range(2, parts)]

    def lanes(source, target):
        return [(2 * source + lane, 2 * target + lane) for lane in range(2)]

    border = lax.all_gather(factor, "col", axis=1, tiled=True)
    first = border[:, :block]
    kernel = kernel_rows(train_x, test_x / scales, scales)
    width = kernel.shape[1] // CHUNKS
    kernels = [kernel[:, c * width : (c + 1) * width] for c in range(CHUNKS)]

    whites, solved, sums = [], [], []
    arrived = []
    for c in range(CHUNKS):
        start = product(inverses, kernels[c])
        from_zero = lax.ppermute(start, "row", [(0, 1)])
        second = product(inverses, kernels[c] - product(first, from_zero))
        moving = jnp.where(even, start, second)
        mine = jnp.zeros_like(moving)
        for hop in range(pairs - 1):
            moving = lax.ppermute(moving, "row", lanes(hop, hop + 1))
            mine = mine + moving
        arrived.append((from_zero, mine))
    for c in range(CHUNKS):
        from_zero, mine = arrived[c]
        other = lax.ppermute(mine, "row", swap)
        panel0 = jnp.where(head, from_zero, jnp.where(even, mine, other))
        panel1 = jnp.where(even, other, mine)
        panels = jnp.concatenate([panel0, panel1], axis=0)
        white = product(inverses, kernels[c] - product(border, panels))
        back = transposed_product(inverses, white)
        terms = transposed_product(border, jnp.where(head, 0.0, back))
        terms0, terms1 = terms[:block], terms[block:]
        sent = lax.ppermute(jnp.where(even, terms1, terms0), "row", swap)
        total = jnp.where(even, terms0, terms1) + sent
        for hop in range(pairs - 1, 0, -1):
            total = total + lax.ppermute(total, "row", lanes(hop, hop - 1))
        whites.append(white)
        solved.append(back)
        sums.append(total)
    outs = []
    for c in range(CHUNKS):
        rest = whites[c] - sums[c]
        last = transposed_product(inverses, rest)
        to_zero = lax.ppermute(transposed_product(first, last), "row", [(1, 0)])
        final = transposed_product(inverses, rest - to_zero)
        outs.append(jnp.where(head, final, solved[c]))
    back_solved = jnp.concatenate(outs, axis=1)
    squares = jnp.concatenate([jnp.sum(w * w, axis=0) for w in whites])
    weighted = jnp.sum(targets[:, None] * back_solved, axis=0)
    explained, mean = lax.psum((squares, weighted), "row")
    return (back_solved, explained / (block * parts), mean)


def solution(mesh):
    placed = (P("row", None), P("col", None), P(), P("row"), P("row", "col"), P("row", None))
    return jax.shard_map(
        local,
        mesh=mesh,
        in_specs=placed,
        out_specs=(P("row", "col"), P("col"), P("col")),
        check_vma=False,
    )
```

time: 885 us -> 606 us (0.68)
  waiting for transfers between devices: 625 us -> 196 us
  starting transfers between devices: 0.21 us -> 202 us
  matrix products: 206 us -> 140 us
  other arithmetic: 2.19 us -> 19.5 us
    psum x4 -> x0, waiting for transfers between devices: 625 us -> none  [the longest x2 314 us: from_root(): return lax.psum(jnp.where(mine, array, jnp.zeros_like(array)), axis)]
    ppermute x0 -> x40, starting transfers between devices: none -> 202 us  [the longest x12 158 us: local(): total = total + lax.ppermute(total, 'row', lanes(hop, hop - 1))]
    ppermute x0 -> x40, waiting for transfers between devices: none -> 173 us  [the longest x12 93.1 us: local(): total = total + lax.ppermute(total, 'row', lanes(hop, hop - 1))]
    dot_general x6 -> x20, matrix products: 116 us -> 80.1 us  [product(): return jnp.dot(left, right, precision=lax.Precision.HIGH)]
    dot_general x5 -> x20, matrix products: 83.3 us -> 54.4 us  [transposed_product(): lax.dot_general(left, right, (((0,), (0,)), ((), ())), precision=lax.Prec...]
    all_gather x1, waiting for transfers between devices: 0.01 us -> 22.1 us  [local(): border = lax.all_gather(factor, 'col', axis=1, tiled=True)]
    add x0 -> x16, other arithmetic: none -> 10.1 us  [the longest x4 7.61 us: local(): mine = mine + moving]
  transfers between devices with their start and end apart: 5 -> 41, of which waited for: 4 -> 11; matrix products, arithmetic and copies ran while one was open for 0% -> 23% of each run, Pallas kernels for 0% -> 0%
where the time goes in v1:
time: 606 us; the launch traced here: 597 us
  starting transfers between devices  202 us (33%)
  waiting for transfers between devices  196 us (32%)
  matrix products  140 us (23%)
  other arithmetic  19.5 us (3%)
  blocking collectives  17.9 us (3%)
  between operations  15.5 us (3%)
  local copies, waits for them, and re-layouts  6.36 us (1%)
    ppermute x12, starting transfers between devices, local(): total = total + lax.ppermute(total, 'row', lanes(hop, hop - 1))  158 us
    ppermute x12, waiting for transfers between devices, local(): total = total + lax.ppermute(total, 'row', lanes(hop, hop - 1))  93.1 us
    dot_general x20, matrix products, product(): return jnp.dot(left, right, precision=lax.Precision.HIGH)  80.1 us
    dot_general x20, matrix products, transposed_product(): lax.dot_general(left, right, (((0,), (0,)), ((), ())), precision=lax.Prec...  54.4 us
    ppermute x12, waiting for transfers between devices, local(): moving = lax.ppermute(moving, 'row', lanes(hop, hop + 1))  46.8 us
    all_gather x1, waiting for transfers between devices, local(): border = lax.all_gather(factor, 'col', axis=1, tiled=True)  22.1 us
    ppermute x12, starting transfers between devices, local(): moving = lax.ppermute(moving, 'row', lanes(hop, hop + 1))  19.9 us
    psum x1, blocking collectives, local(): explained, mean = lax.psum((squares, weighted), 'row')  17.9 us
  transfers between devices with their start and end apart: 41, of which 11 were waited for; matrix products, arithmetic and copies ran while one was open for 23% of the time, Pallas kernels for 0%

profile of v1, /device:TPU:0, one launch (start us, length us, event | category | flops | bytes accessed | tf_op | source)
XLA Modules:
  0.0 597.1 jit_solution(2922562838566015884)
XLA Ops:
  9.5 5.6 multiply_exponential_fusion
  15.1 4.6 convolution_bitcast_fusion.11
  19.7 5.8 collective-permute-start
  25.6 4.6 convolution_bitcast_fusion.9
  31.7 4.6 convolution_bitcast_fusion.7
  37.7 4.6 convolution_bitcast_fusion.5
  44.1 4.4 collective-permute-done
  48.4 22.1 %all-gather.2.cloned.1.call-done = f32[1024,2048]{1,0:T(8,128)} async-done(((f32[1024,512]{1,0:T(8,128)}), f32[1024,2048]{1,0:T(8,128)}) %all-gather.2.cloned.1.call-update) | async-done | bytes 8388624 | tf_op jit(solution)/shard_map/all_gather | solution.py:39
  70.6 4.8 fusion.47
  75.4 5.6 fusion.87
  87.7 5.1 fusion.85
  97.2 4.9 fusion.83
  103.4 11.3 %collective-permute-done.30 = f32[1024,256]{0,1:T(8,128)S(1)} collective-permute-done((f32[1024,256]{0,1:T(8,128)}, f32[1024,256]{0,1:T(8,128)S(1)}, u32[]{:S(2)}, u32[]{:S(2)}) %collective-permute-start.30) | collective-permute-done | bytes 1048608 | tf_op jit(solution)/shard_map/ppermute | solution.py:49
  116.6 4.9 fusion.81
  123.6 6.7 %collective-permute-done.11 = f32[1024,256]{0,1:T(8,128)} collective-permute-done((f32[1024,256]{0,1:T(8,128)S(1)}, f32[1024,256]{0,1:T(8,128)}, u32[]{:S(2)}, u32[]{:S(2)}) %collective-permute-start.11) | collective-permute-done | bytes 1048608 | tf_op jit(solution)/shard_map/ppermute | solution.py:54
  132.0 20.8 %collective-permute-done.21 = f32[1024,256]{0,1:T(8,128)S(1)} collective-permute-done((f32[1024,256]{0,1:T(8,128)S(1)}, f32[1024,256]{0,1:T(8,128)S(1)}, u32[]{:S(2)}, u32[]{:S(2)}) %collective-permute-start.21) | collective-permute-done | bytes 1048608 | tf_op jit(solution)/shard_map/ppermute | solution.py:54
  155.4 19.2 %collective-permute-done.31 = f32[1024,256]{0,1:T(8,128)S(1)} collective-permute-done((f32[1024,256]{0,1:T(8,128)S(1)}, f32[1024,256]{0,1:T(8,128)S(1)}, u32[]{:S(2)}, u32[]{:S(2)}) %collective-permute-start.31) | collective-permute-done | bytes 1048608 | tf_op jit(solution)/shard_map/ppermute | solution.py:54
  207.6 3.9 fusion.102
  219.5 3.8 fusion.97
  223.3 3.7 fusion.100
  229.3 4.4 convolution_bitcast_fusion.3
  238.2 4.4 convolution_bitcast_fusion.2
  245.8 4.4 convolution_bitcast_fusion.1
  253.6 4.4 convolution_bitcast_fusion
  262.3 147.9 %collective-permute-start.36 = (f32[1024,256]{0,1:T(8,128)S(1)}, f32[1024,256]{0,1:T(8,128)S(1)}, u32[]{:S(2)}, u32[]{:S(2)}) collective-permute-start(f32[1024,256]{0,1:T(8,128)S(1)} %select_add_fusion), channel_id=1, source_target_pairs={{24,16},{28,20},{25,17},{29,21},{26,18},{30,22},{27,19},{31,23}} | collective-permute-start | bytes 3145736 | tf_op jit(solution)/shard_map/ppermute | solution.py:70
  420.0 43.5 %collective-permute-done.8 = f32[1024,256]{0,1:T(8,128)S(1)} collective-permute-done((f32[1024,256]{0,1:T(8,128)S(1)}, f32[1024,256]{0,1:T(8,128)S(1)}, u32[]{:S(2)}, u32[]{:S(2)}) %collective-permute-start.8) | collective-permute-done | bytes 1048608 | tf_op jit(solution)/shard_map/ppermute | solution.py:70
  469.3 16.6 %collective-permute-done.18 = f32[1024,256]{0,1:T(8,128)S(1)} collective-permute-done((f32[1024,256]{0,1:T(8,128)S(1)}, f32[1024,256]{0,1:T(8,128)S(1)}, u32[]{:S(2)}, u32[]{:S(2)}) %collective-permute-start.18) | collective-permute-done | bytes 1048608 | tf_op jit(solution)/shard_map/ppermute | solution.py:70
  491.8 16.6 %collective-permute-done.28 = f32[1024,256]{0,1:T(8,128)S(1)} collective-permute-done((f32[1024,256]{0,1:T(8,128)S(1)}, f32[1024,256]{0,1:T(8,128)S(1)}, u32[]{:S(2)}, u32[]{:S(2)}) %collective-permute-start.28) | collective-permute-done | bytes 1048608 | tf_op jit(solution)/shard_map/ppermute | solution.py:70
  514.5 16.4 %collective-permute-done.38 = f32[1024,256]{0,1:T(8,128)S(1)} collective-permute-done((f32[1024,256]{0,1:T(8,128)S(1)}, f32[1024,256]{0,1:T(8,128)S(1)}, u32[]{:S(2)}, u32[]{:S(2)}) %collective-permute-start.38) | collective-permute-done | bytes 1048608 | tf_op jit(solution)/shard_map/ppermute | solution.py:70
  544.0 17.2 %collective-permute-done.39 = f32[1024,256]{0,1:T(8,128)S(1)} collective-permute-done((f32[1024,256]{0,1:T(8,128)S(1)}, f32[1024,256]{0,1:T(8,128)S(1)}, u32[]{:S(2)}, u32[]{:S(2)}) %collective-permute-start.39) | collective-permute-done | bytes 1048608 | tf_op jit(solution)/shard_map/ppermute | solution.py:78
  566.0 17.9 %all-reduce = (f32[1024]{0:T(1024)S(1)}, f32[1024]{0:T(1024)}) all-reduce(f32[1024]{0:T(1024)S(1)} %pad_maximum_fusion.1, f32[1024]{0:T(1024)S(1)} %get-tuple-element.10), channel_id=1, replica_groups=mesh['row'=8,'col'=4] {'row'}, use_global_device_ids=true, to_apply=%region_6.7 | all-reduce | flops 2048 | bytes 16384 | tf_op jit(solution)/shard_map/psum | solution.py:84
  584.5 5.3 copy.9
  (151 shorter events, 131.6 us)
Async XLA Ops:
  7.2 63.4 %all-gather.2.cloned.1.call-start = ((), (), s32[]{:S(2)}) async-start(), calls=%async_computation | async-start | bytes 10485760 | tf_op jit(solution)/shard_map/all_gather | solution.py:39
  19.7 28.7 %collective-permute-start = (f32[1024,256]{0,1:T(8,128)}, f32[1024,256]{0,1:T(8,128)}, u32[]{:S(2)}, u32[]{:S(2)}) collective-permute-start(f32[1024,256]{0,1:T(8,128)} %convolution_bitcast_fusion.11), channel_id=1, source_target_pairs={{0,4},{1,5},{2,6},{3,7}} | collective-permute-start | bytes 3145736 | tf_op jit(solution)/shard_map/ppermute | solution.py:49
  30.2 54.3 %collective-permute-start.10 = (f32[1024,256]{0,1:T(8,128)}, f32[1024,256]{0,1:T(8,128)S(1)}, u32[]{:S(2)}, u32[]{:S(2)}) collective-permute-start(f32[1024,256]{0,1:T(8,128)} %convolution_bitcast_fusion.9), channel_id=1, source_target_pairs={{0,4},{1,5},{2,6},{3,7}} | collective-permute-start | bytes 3145736 | tf_op jit(solution)/shard_map/ppermute | solution.py:49
  36.3 58.9 %collective-permute-start.20 = (f32[1024,256]{0,1:T(8,128)}, f32[1024,256]{0,1:T(8,128)S(1)}, u32[]{:S(2)}, u32[]{:S(2)}) collective-permute-start(f32[1024,256]{0,1:T(8,128)} %convolution_bitcast_fusion.7), channel_id=1, source_target_pairs={{0,4},{1,5},{2,6},{3,7}} | collective-permute-start | bytes 3145736 | tf_op jit(solution)/shard_map/ppermute | solution.py:49
  42.3 72.4 %collective-permute-start.30 = (f32[1024,256]{0,1:T(8,128)}, f32[1024,256]{0,1:T(8,128)S(1)}, u32[]{:S(2)}, u32[]{:S(2)}) collective-permute-start(f32[1024,256]{0,1:T(8,128)} %convolution_bitcast_fusion.5), channel_id=1, source_target_pairs={{0,4},{1,5},{2,6},{3,7}} | collective-permute-start | bytes 3145736 | tf_op jit(solution)/shard_map/ppermute | solution.py:49
  81.0 41.9 %collective-permute-start.1 = (f32[1024,256]{0,1:T(8,128)S(1)}, f32[1024,256]{0,1:T(8,128)S(1)}, u32[]{:S(2)}, u32[]{:S(2)}) collective-permute-start(f32[1024,256]{0,1:T(8,128)S(1)} %fusion.87), channel_id=1, source_target_pairs={{0,8},{4,12},{1,9},{5,13},{2,10},{6,14},{3,11},{7,15}} | collective-permute-start | bytes 3145736 | tf_op jit(solution)/shard_map/ppermute | solution.py:54
  92.7 37.6 %collective-permute-start.11 = (f32[1024,256]{0,1:T(8,128)S(1)}, f32[1024,256]{0,1:T(8,128)}, u32[]{:S(2)}, u32[]{:S(2)}) collective-permute-start(f32[1024,256]{0,1:T(8,128)S(1)} %fusion.85), channel_id=1, source_target_pairs={{0,8},{4,12},{1,9},{5,13},{2,10},{6,14},{3,11},{7,15}} | collective-permute-start | bytes 3145736 | tf_op jit(solution)/shard_map/ppermute | solution.py:54
  102.1 50.8 %collective-permute-start.21 = (f32[1024,256]{0,1:T(8,128)S(1)}, f32[1024,256]{0,1:T(8,128)S(1)}, u32[]{:S(2)}, u32[]{:S(2)}) collective-permute-start(f32[1024,256]{0,1:T(8,128)S(1)} %fusion.83), channel_id=1, source_target_pairs={{0,8},{4,12},{1,9},{5,13},{2,10},{6,14},{3,11},{7,15}} | collective-permute-start | bytes 3145736 | tf_op jit(solution)/shard_map/ppermute | solution.py:54
  121.5 53.1 %collective-permute-start.31 = (f32[1024,256]{0,1:T(8,128)S(1)}, f32[1024,256]{0,1:T(8,128)S(1)}, u32[]{:S(2)}, u32[]{:S(2)}) collective-permute-start(f32[1024,256]{0,1:T(8,128)S(1)} %fusion.81), channel_id=1, source_target_pairs={{0,8},{4,12},{1,9},{5,13},{2,10},{6,14},{3,11},{7,15}} | collective-permute-start | bytes 3145736 | tf_op jit(solution)/shard_map/ppermute | solution.py:54
  122.9 53.4 %collective-permute-start.2 = (f32[1024,256]{0,1:T(8,128)S(1)}, f32[1024,256]{0,1:T(8,128)S(1)}, u32[]{:S(2)}, u32[]{:S(2)}) collective-permute-start(f32[1024,256]{0,1:T(8,128)S(1)} %collective-permute-done.1), channel_id=1, source_target_pairs={{8,16},{12,20},{9,17},{13,21},{10,18},{14,22},{11,19},{15,23}} | collective-permute-start | bytes 3145736 | tf_op jit(solution)/shard_map/ppermute | solution.py:54
  130.4 46.6 %collective-permute-start.12 = (f32[1024,256]{0,1:T(8,128)}, f32[1024,256]{0,1:T(8,128)}, u32[]{:S(2)}, u32[]{:S(2)}) collective-permute-start(f32[1024,256]{0,1:T(8,128)} %collective-permute-done.11), channel_id=1, source_target_pairs={{8,16},{12,20},{9,17},{13,21},{10,18},{14,22},{11,19},{15,23}} | collective-permute-start | bytes 3145736 | tf_op jit(solution)/shard_map/ppermute | solution.py:54
  153.8 24.9 %collective-permute-start.22 = (f32[1024,256]{0,1:T(8,128)S(1)}, f32[1024,256]{0,1:T(8,128)}, u32[]{:S(2)}, u32[]{:S(2)}) collective-permute-start(f32[1024,256]{0,1:T(8,128)S(1)} %collective-permute-done.21), channel_id=1, source_target_pairs={{8,16},{12,20},{9,17},{13,21},{10,18},{14,22},{11,19},{15,23}} | collective-permute-start | bytes 3145736 | tf_op jit(solution)/shard_map/ppermute | solution.py:54
  180.3 10.5 %collective-permute-start.33 = (f32[1024,256]{0,1:T(8,128)}, f32[1024,256]{0,1:T(8,128)}, u32[]{:S(2)}, u32[]{:S(2)}) collective-permute-start(f32[1024,256]{0,1:T(8,128)} %collective-permute-done.32), channel_id=1, source_target_pairs={{16,24},{20,28},{17,25},{21,29},{18,26},{22,30},{19,27},{23,31}} | collective-permute-start | bytes 3145736 | tf_op jit(solution)/shard_map/ppermute | solution.py:54
  183.3 10.9 %collective-permute-start.4 = (f32[1024,256]{0,1:T(8,128)}, f32[1024,256]{0,1:T(8,128)}, u32[]{:S(2)}, u32[]{:S(2)}) collective-permute-start(f32[1024,256]{0,1:T(8,128)} %add_add_fusion.3), channel_id=1, source_target_pairs={{8,12},{12,8},{16,20},{20,16},{24,28},{28,24},{9,13},{13,9},{17,21... | collective-permute-start | bytes 3145736 | tf_op jit(solution)/shard_map/ppermute | solution.py:59
  187.2 16.5 %collective-permute-start.14 = (f32[1024,256]{0,1:T(8,128)S(1)}, f32[1024,256]{0,1:T(8,128)S(1)}, u32[]{:S(2)}, u32[]{:S(2)}) collective-permute-start(f32[1024,256]{0,1:T(8,128)S(1)} %add_add_fusion.2), channel_id=1, source_target_pairs={{8,12},{12,8},{16,20},{20,16},{24,28},{28,24},{9,13},{13,9},{17,21... | collective-permute-start | bytes 3145736 | tf_op jit(solution)/shard_map/ppermute | solution.py:59
  189.9 21.6 %collective-permute-start.24 = (f32[1024,256]{0,1:T(8,128)S(1)}, f32[1024,256]{0,1:T(8,128)S(1)}, u32[]{:S(2)}, u32[]{:S(2)}) collective-permute-start(f32[1024,256]{0,1:T(8,128)S(1)} %add_add_fusion.1), channel_id=1, source_target_pairs={{8,12},{12,8},{16,20},{20,16},{24,28},{28,24},{9,13},{13,9},{17,21... | collective-permute-start | bytes 3145736 | tf_op jit(solution)/shard_map/ppermute | solution.py:59
  193.0 26.1 %collective-permute-start.34 = (f32[1024,256]{0,1:T(8,128)S(1)}, f32[1024,256]{0,1:T(8,128)S(1)}, u32[]{:S(2)}, u32[]{:S(2)}) collective-permute-start(f32[1024,256]{0,1:T(8,128)S(1)} %add_add_fusion), channel_id=1, source_target_pairs={{8,12},{12,8},{16,20},{20,16},{24,28},{28,24},{9,13},{13,9},{17,21... | collective-permute-start | bytes 3145736 | tf_op jit(solution)/shard_map/ppermute | solution.py:59
  234.8 24.1 %collective-permute-start.5 = (f32[1024,256]{0,1:T(8,128)}, f32[1024,256]{0,1:T(8,128)S(1)}, u32[]{:S(2)}, u32[]{:S(2)}) collective-permute-start(f32[1024,256]{0,1:T(8,128)} %slice_select_fusion.3), channel_id=1, source_target_pairs={{8,12},{12,8},{16,20},{20,16},{24,28},{28,24},{9,13},{13,9},{17,21... | collective-permute-start | bytes 3145736 | tf_op jit(solution)/shard_map/ppermute | solution.py:67
  242.8 17.1 %collective-permute-start.15 = (f32[1024,256]{0,1:T(8,128)S(1)}, f32[1024,256]{0,1:T(8,128)S(1)}, u32[]{:S(2)}, u32[]{:S(2)}) collective-permute-start(f32[1024,256]{0,1:T(8,128)S(1)} %slice_select_fusion.2), channel_id=1, source_target_pairs={{8,12},{12,8},{16,20},{20,16},{24,28},{28,24},{9,13},{13,9},{17,21... | collective-permute-start | bytes 3145736 | tf_op jit(solution)/shard_map/ppermute | solution.py:67
  250.4 10.6 %collective-permute-start.25 = (f32[1024,256]{0,1:T(8,128)S(1)}, f32[1024,256]{0,1:T(8,128)S(1)}, u32[]{:S(2)}, u32[]{:S(2)}) collective-permute-start(f32[1024,256]{0,1:T(8,128)S(1)} %slice_select_fusion.1), channel_id=1, source_target_pairs={{8,12},{12,8},{16,20},{20,16},{24,28},{28,24},{9,13},{13,9},{17,21... | collective-permute-start | bytes 3145736 | tf_op jit(solution)/shard_map/ppermute | solution.py:67
  259.1 151.1 %collective-permute-start.6 = (f32[1024,256]{0,1:T(8,128)S(1)}, f32[1024,256]{0,1:T(8,128)S(1)}, u32[]{:S(2)}, u32[]{:S(2)}) collective-permute-start(f32[1024,256]{0,1:T(8,128)S(1)} %select_add_fusion.3), channel_id=1, source_target_pairs={{24,16},{28,20},{25,17},{29,21},{26,18},{30,22},{27,19},{31,23}} | collective-permute-start | bytes 3145736 | tf_op jit(solution)/shard_map/ppermute | solution.py:70
  260.2 150.9 %collective-permute-start.16 = (f32[1024,256]{0,1:T(8,128)S(1)}, f32[1024,256]{0,1:T(8,128)S(1)}, u32[]{:S(2)}, u32[]{:S(2)}) collective-permute-start(f32[1024,256]{0,1:T(8,128)S(1)} %select_add_fusion.2), channel_id=1, source_target_pairs={{24,16},{28,20},{25,17},{29,21},{26,18},{30,22},{27,19},{31,23}} | collective-permute-start | bytes 3145736 | tf_op jit(solution)/shard_map/ppermute | solution.py:70
  261.3 150.7 %collective-permute-start.26 = (f32[1024,256]{0,1:T(8,128)S(1)}, f32[1024,256]{0,1:T(8,128)S(1)}, u32[]{:S(2)}, u32[]{:S(2)}) collective-permute-start(f32[1024,256]{0,1:T(8,128)S(1)} %select_add_fusion.1), channel_id=1, source_target_pairs={{24,16},{28,20},{25,17},{29,21},{26,18},{30,22},{27,19},{31,23}} | collective-permute-start | bytes 3145736 | tf_op jit(solution)/shard_map/ppermute | solution.py:70
  262.3 150.6 %collective-permute-start.36 = (f32[1024,256]{0,1:T(8,128)S(1)}, f32[1024,256]{0,1:T(8,128)S(1)}, u32[]{:S(2)}, u32[]{:S(2)}) collective-permute-start(f32[1024,256]{0,1:T(8,128)S(1)} %select_add_fusion), channel_id=1, source_target_pairs={{24,16},{28,20},{25,17},{29,21},{26,18},{30,22},{27,19},{31,23}} | collective-permute-start | bytes 3145736 | tf_op jit(solution)/shard_map/ppermute | solution.py:70
  414.1 49.4 %collective-permute-start.8 = (f32[1024,256]{0,1:T(8,128)S(1)}, f32[1024,256]{0,1:T(8,128)S(1)}, u32[]{:S(2)}, u32[]{:S(2)}) collective-permute-start(f32[1024,256]{0,1:T(8,128)S(1)} %add.101), channel_id=1, source_target_pairs={{8,0},{12,4},{9,1},{13,5},{10,2},{14,6},{11,3},{15,7}} | collective-permute-start | bytes 3145736 | tf_op jit(solution)/shard_map/ppermute | solution.py:70
  415.5 70.4 %collective-permute-start.18 = (f32[1024,256]{0,1:T(8,128)S(1)}, f32[1024,256]{0,1:T(8,128)S(1)}, u32[]{:S(2)}, u32[]{:S(2)}) collective-permute-start(f32[1024,256]{0,1:T(8,128)S(1)} %add.107), channel_id=1, source_target_pairs={{8,0},{12,4},{9,1},{13,5},{10,2},{14,6},{11,3},{15,7}} | collective-permute-start | bytes 3145736 | tf_op jit(solution)/shard_map/ppermute | solution.py:70
  417.0 91.4 %collective-permute-start.28 = (f32[1024,256]{0,1:T(8,128)S(1)}, f32[1024,256]{0,1:T(8,128)S(1)}, u32[]{:S(2)}, u32[]{:S(2)}) collective-permute-start(f32[1024,256]{0,1:T(8,128)S(1)} %add.113), channel_id=1, source_target_pairs={{8,0},{12,4},{9,1},{13,5},{10,2},{14,6},{11,3},{15,7}} | collective-permute-start | bytes 3145736 | tf_op jit(solution)/shard_map/ppermute | solution.py:70
  418.5 112.4 %collective-permute-start.38 = (f32[1024,256]{0,1:T(8,128)S(1)}, f32[1024,256]{0,1:T(8,128)S(1)}, u32[]{:S(2)}, u32[]{:S(2)}) collective-permute-start(f32[1024,256]{0,1:T(8,128)S(1)} %add.119), channel_id=1, source_target_pairs={{8,0},{12,4},{9,1},{13,5},{10,2},{14,6},{11,3},{15,7}} | collective-permute-start | bytes 3145736 | tf_op jit(solution)/shard_map/ppermute | solution.py:70
  468.0 68.8 %collective-permute-start.9 = (f32[1024,256]{0,1:T(8,128)S(1)}, f32[1024,256]{0,1:T(8,128)S(1)}, u32[]{:S(2)}, u32[]{:S(2)}) collective-permute-start(f32[1024,256]{0,1:T(8,128)S(1)} %fusion.50), channel_id=1, source_target_pairs={{4,0},{5,1},{6,2},{7,3}} | collective-permute-start | bytes 3145736 | tf_op jit(solution)/shard_map/ppermute | solution.py:78
  490.5 48.6 %collective-permute-start.19 = (f32[1024,256]{0,1:T(8,128)S(1)}, f32[1024,256]{0,1:T(8,128)S(1)}, u32[]{:S(2)}, u32[]{:S(2)}) collective-permute-start(f32[1024,256]{0,1:T(8,128)S(1)} %fusion.59), channel_id=1, source_target_pairs={{4,0},{5,1},{6,2},{7,3}} | collective-permute-start | bytes 3145736 | tf_op jit(solution)/shard_map/ppermute | solution.py:78
  513.0 28.6 %collective-permute-start.29 = (f32[1024,256]{0,1:T(8,128)S(1)}, f32[1024,256]{0,1:T(8,128)S(1)}, u32[]{:S(2)}, u32[]{:S(2)}) collective-permute-start(f32[1024,256]{0,1:T(8,128)S(1)} %fusion.68), channel_id=1, source_target_pairs={{4,0},{5,1},{6,2},{7,3}} | collective-permute-start | bytes 3145736 | tf_op jit(solution)/shard_map/ppermute | solution.py:78
  535.5 25.6 %collective-permute-start.39 = (f32[1024,256]{0,1:T(8,128)S(1)}, f32[1024,256]{0,1:T(8,128)S(1)}, u32[]{:S(2)}, u32[]{:S(2)}) collective-permute-start(f32[1024,256]{0,1:T(8,128)S(1)} %fusion.77), channel_id=1, source_target_pairs={{4,0},{5,1},{6,2},{7,3}} | collective-permute-start | bytes 3145736 | tf_op jit(solution)/shard_map/ppermute | solution.py:78
  (23 other events, 170.7 us)
Sparse Core Ops, SparseCore 0:
  9.6 60.9 all-gather.1

commit v2 on v1

--- a/solution.py
+++ b/solution.py
@@ -42,21 +42,63 @@
     width = kernel.shape[1] // CHUNKS
     kernels = [kernel[:, c * width : (c + 1) * width] for c in range(CHUNKS)]
 
+    pair = position // 2
     whites, solved, sums = [], [], []
-    arrived = []
+    zeros, moving = [], []
     for c in range(CHUNKS):
         start = product(inverses, kernels[c])
-        from_zero = lax.ppermute(start, "row", [(0, 1)])
-        second = product(inverses, kernels[c] - product(first, from_zero))
-        moving = jnp.where(even, start, second)
-        mine = jnp.zeros_like(moving)
-        for hop in range(pairs - 1):
-            moving = lax.ppermute(moving, "row", lanes(hop, hop + 1))
-            mine = mine + moving
-        arrived.append((from_zero, mine))
+        zeros.append(lax.ppermute(start, "row", [(0, 1)]))
+        second = product(inverses, kernels[c] - product(first, zeros[c]))
+        moving.append(jnp.where(even, start, second))
+    arrived = [None] * CHUNKS
+    others = {}
+
+    def exchange(c):
+        others[c] = lax.ppermute(arrived[c], "row", swap)
+
+    got = None
+    for step in range(CHUNKS + pairs - 2):
+        active = [(p, step - p) for p in range(pairs - 1) if 0 <= step - p < CHUNKS]
+        if got is None:
+            sent = moving[step]
+        elif step < CHUNKS:
+            sent = jnp.where(pair == 0, moving[step], got)
+        else:
+            sent = got
+        done = step - pairs
+        if done in others:
+            sent, others[done] = lax.optimization_barrier((sent, others[done]))
+        got = lax.ppermute(sent, "row", [link for p, _ in active for link in lanes(p, p + 1)])
+        for p, c in active:
+            part = jnp.where(pair == p + 1, got, 0.0)
+            arrived[c] = part if arrived[c] is None else arrived[c] + part
+            if p == pairs - 2 and c < 2:
+                exchange(c)
+    def hop(step):
+        active = [(p, step - (pairs - 1 - p)) for p in range(1, pairs)]
+        active = [(p, c) for p, c in active if 0 <= c < CHUNKS]
+        sent = sums[active[-1][1]]
+        for p, c in active[:-1]:
+            sent = jnp.where(pair == p, sums[c], sent)
+        if step + 2 < CHUNKS:
+            sent, others[step + 2] = lax.optimization_barrier((sent, others[step + 2]))
+        got = lax.ppermute(sent, "row", [link for p, _ in active for link in lanes(p, p - 1)])
+        for p, c in active:
+            sums[c] = sums[c] + jnp.where(pair == p - 1, got, 0.0)
+            if p == 1:
+                finish(c)
+
+    def finish(c):
+        rest = whites[c] - sums[c]
+        last = transposed_product(inverses, rest)
+        to_zero = lax.ppermute(transposed_product(first, last), "row", [(1, 0)])
+        final = transposed_product(inverses, rest - to_zero)
+        outs.append(jnp.where(head, final, solved[c]))
+
+    outs = []
     for c in range(CHUNKS):
-        from_zero, mine = arrived[c]
-        other = lax.ppermute(mine, "row", swap)
+        from_zero, mine = zeros[c], arrived[c]
+        other = others[c]
         panel0 = jnp.where(head, from_zero, jnp.where(even, mine, other))
         panel1 = jnp.where(even, other, mine)
         panels = jnp.concatenate([panel0, panel1], axis=0)
@@ -64,20 +106,19 @@
         back = transposed_product(inverses, white)
         terms = transposed_product(border, jnp.where(head, 0.0, back))
         terms0, terms1 = terms[:block], terms[block:]
-        sent = lax.ppermute(jnp.where(even, terms1, terms0), "row", swap)
-        total = jnp.where(even, terms0, terms1) + sent
-        for hop in range(pairs - 1, 0, -1):
-            total = total + lax.ppermute(total, "row", lanes(hop, hop - 1))
+        sent = jnp.where(even, terms1, terms0)
+        if c + 2 < CHUNKS:
+            sent, arrived[c + 2] = lax.optimization_barrier((sent, arrived[c + 2]))
+        got = lax.ppermute(sent, "row", swap)
+        if c + 2 < CHUNKS:
+            exchange(c + 2)
         whites.append(white)
         solved.append(back)
-        sums.append(total)
-    outs = []
-    for c in range(CHUNKS):
-        rest = whites[c] - sums[c]
-        last = transposed_product(inverses, rest)
-        to_zero = lax.ppermute(transposed_product(first, last), "row", [(1, 0)])
-        final = transposed_product(inverses, rest - to_zero)
-        outs.append(jnp.where(head, final, solved[c]))
+        sums.append(jnp.where(even, terms0, terms1) + got)
+        if c >= 1:
+            hop(c - 1)
+    for step in range(CHUNKS - 1, CHUNKS + pairs - 2):
+        hop(step)
     back_solved = jnp.concatenate(outs, axis=1)
     squares = jnp.concatenate([jnp.sum(w * w, axis=0) for w in whites])
     weighted = jnp.sum(targets[:, None] * back_solved, axis=0)

time: 606 us -> 593 us (0.979)
  starting transfers between devices: 202 us -> 56.6 us
  waiting for transfers between devices: 196 us -> 315 us
  other arithmetic: 19.5 us -> 30 us
    ppermute x40 -> x28, starting transfers between devices: 202 us -> 56.6 us  [the longest x6 21.2 us: local(): lax.ppermute(sent, 'row', [link for p, _ in active for link in lanes(p, p...]
    ppermute x40 -> x28, waiting for transfers between devices: 173 us -> 291 us  [the longest x6 186 us: hop(): lax.ppermute(sent, 'row', [link for p, _ in active for link in lanes(p, p...]
    select_n x4 -> x7, other arithmetic: 1.62 us -> 10.4 us  [the longest x3 7.85 us: hop(): sent = jnp.where(pair == p, sums[c], sent)]
  transfers between devices with their start and end apart: 41 -> 29, of which waited for: 11 -> 13; matrix products, arithmetic and copies ran while one was open for 23% -> 26% of each run, Pallas kernels for 0% -> 0%
where the time goes in v2:
time: 593 us; the launch traced here: 583 us
  waiting for transfers between devices  315 us (53%)
  matrix products  143 us (24%)
  starting transfers between devices  56.6 us (10%)
  other arithmetic  30 us (5%)
  blocking collectives  17.9 us (3%)
  between operations  15.5 us (3%)
    ppermute x6, waiting for transfers between devices, hop(): lax.ppermute(sent, 'row', [link for p, _ in active for link in lanes(p, p...  186 us
    dot_general x20, matrix products, product(): return jnp.dot(left, right, precision=lax.Precision.HIGH)  82.4 us
    ppermute x6, waiting for transfers between devices, local(): lax.ppermute(sent, 'row', [link for p, _ in active for link in lanes(p, p...  59.1 us
    dot_general x20, matrix products, transposed_product(): lax.dot_general(left, right, (((0,), (0,)), ((), ())), precision=lax.Prec...  54.7 us
    ppermute x4, waiting for transfers between devices, finish(): to_zero = lax.ppermute(transposed_product(first, last), 'row', [(1, 0)])  29 us
    all_gather x1, waiting for transfers between devices, local(): border = lax.all_gather(factor, 'col', axis=1, tiled=True)  23.4 us
    ppermute x6, starting transfers between devices, local(): lax.ppermute(sent, 'row', [link for p, _ in active for link in lanes(p, p...  21.2 us
    psum x1, blocking collectives, local(): explained, mean = lax.psum((squares, weighted), 'row')  17.9 us
  transfers between devices with their start and end apart: 29, of which 13 were waited for; matrix products, arithmetic and copies ran while one was open for 26% of the time, Pallas kernels for 0%

profile of v2, /device:TPU:0, one launch (start us, length us, event | category | flops | bytes accessed | tf_op | source)
XLA Modules:
  0.0 583.5 jit_solution(16028199928164791825)
XLA Ops:
  9.5 5.6 multiply_exponential_fusion
  18.7 4.9 collective-permute-start
  23.7 4.6 convolution_bitcast_fusion.9
  29.9 17.3 %collective-permute-done = f32[1024,256]{0,1:T(8,128)S(1)} collective-permute-done((f32[1024,256]{0,1:T(8,128)S(1)}, f32[1024,256]{0,1:T(8,128)S(1)}, u32[]{:S(2)}, u32[]{:S(2)}) %collective-permute-start) | collective-permute-done | bytes 1048608 | tf_op jit(solution)/shard_map/ppermute | solution.py:50
  47.2 23.4 %all-gather.2.cloned.1.call-done = f32[1024,2048]{1,0:T(8,128)} async-done(((f32[1024,512]{1,0:T(8,128)}), f32[1024,2048]{1,0:T(8,128)}) %all-gather.2.cloned.1.call-update) | async-done | bytes 8388624 | tf_op jit(solution)/shard_map/all_gather | solution.py:39
  70.6 4.5 fusion.47
  75.1 4.7 fusion.90
  84.1 6.0 %convolution_bitcast_fusion.7 = f32[1024,256]{0,1:T(8,128)} fusion(f32[1024,1024]{1,0:T(8,128)S(1)} %copy-done.1, f32[1024,1024]{1,0:T(8,128)} %copy-done.4), kind=kOutput, calls=%fused_computation.70 | convolution fusion | flops 1610612736 | bytes 6291456 | tf_op jit(solution)/shard_map/dot_general | solution.py:10
  94.0 4.7 fusion.53
  98.8 7.5 %collective-permute-done.1 = f32[1024,256]{0,1:T(8,128)} collective-permute-done((f32[1024,256]{0,1:T(8,128)}, f32[1024,256]{0,1:T(8,128)}, u32[]{:S(2)}, u32[]{:S(2)}) %collective-permute-start.1) | collective-permute-done | bytes 1048608 | tf_op jit(solution)/shard_map/ppermute | solution.py:71
  106.3 4.9 fusion.89
  111.2 4.8 collective-permute-start.3
  125.0 13.0 %collective-permute-done.3 = f32[1024,256]{0,1:T(8,128)S(1)} collective-permute-done((f32[1024,256]{0,1:T(8,128)S(1)}, f32[1024,256]{0,1:T(8,128)S(1)}, u32[]{:S(2)}, u32[]{:S(2)}) %collective-permute-start.3) | collective-permute-done | bytes 1048608 | tf_op jit(solution)/shard_map/ppermute | solution.py:71
  138.0 5.3 fusion.87
  143.3 4.5 collective-permute-start.5
  149.7 19.1 %collective-permute-done.5 = f32[1024,256]{0,1:T(8,128)S(1)} collective-permute-done((f32[1024,256]{0,1:T(8,128)S(1)}, f32[1024,256]{0,1:T(8,128)S(1)}, u32[]{:S(2)}, u32[]{:S(2)}) %collective-permute-start.5) | collective-permute-done | bytes 1048608 | tf_op jit(solution)/shard_map/ppermute | solution.py:71
  168.8 4.7 fusion.85
  173.5 5.4 collective-permute-start.7
  178.9 19.4 %collective-permute-done.7 = f32[1024,256]{0,1:T(8,128)} collective-permute-done((f32[1024,256]{0,1:T(8,128)}, f32[1024,256]{0,1:T(8,128)}, u32[]{:S(2)}, u32[]{:S(2)}) %collective-permute-start.7) | collective-permute-done | bytes 1048608 | tf_op jit(solution)/shard_map/ppermute | solution.py:71
  207.4 6.1 %fusion.91 = f32[1024,256]{1,0:T(8,128)S(1)} fusion(f32[1024,2048]{1,0:T(8,128)} %all-gather.2.cloned.1.call-done, f32[1024,256]{0,1:T(8,128)S(1)} %get-tuple-element.58, f32[1024,256]{0,1:T(8,128)S(1)} %get-tuple-element.57, f32[1024,1024]{1,0:T(8,128)S(1)} %copy-done.6), kind=kOutput, calls=%fused_computation.78 | convolution fusion | flops 3222011904 | bytes 12582912 | tf_op jit(solution)/shard_map/dot_general | solution.py:10
  219.7 4.4 convolution_bitcast_fusion.3
  259.9 4.8 convolution_bitcast_fusion.1
  282.0 4.4 convolution_bitcast_fusion
  289.5 137.6 %collective-permute-done.19 = f32[1024,256]{0,1:T(8,128)S(1)} collective-permute-done((f32[1024,256]{0,1:T(8,128)S(1)}, f32[1024,256]{0,1:T(8,128)S(1)}, u32[]{:S(2)}, u32[]{:S(2)}) %collective-permute-start.19) | collective-permute-done | bytes 1048608 | tf_op jit(solution)/shard_map/ppermute | solution.py:85
  432.5 25.0 %collective-permute-done.22 = f32[1024,256]{0,1:T(8,128)S(1)} collective-permute-done((f32[1024,256]{0,1:T(8,128)}, f32[1024,256]{0,1:T(8,128)S(1)}, u32[]{:S(2)}, u32[]{:S(2)}) %collective-permute-start.22) | collective-permute-done | bytes 1048608 | tf_op jit(solution)/shard_map/ppermute | solution.py:85
  469.9 17.5 %collective-permute-done.24 = f32[1024,256]{0,1:T(8,128)S(1)} collective-permute-done((f32[1024,256]{0,1:T(8,128)S(1)}, f32[1024,256]{0,1:T(8,128)S(1)}, u32[]{:S(2)}, u32[]{:S(2)}) %collective-permute-start.24) | collective-permute-done | bytes 1048608 | tf_op jit(solution)/shard_map/ppermute | solution.py:85
  499.3 5.7 collective-permute-done.26
  513.8 6.1 %collective-permute-done.23 = f32[1024,256]{0,1:T(8,128)S(1)} collective-permute-done((f32[1024,256]{0,1:T(8,128)S(1)}, f32[1024,256]{0,1:T(8,128)S(1)}, u32[]{:S(2)}, u32[]{:S(2)}) %collective-permute-start.23) | collective-permute-done | bytes 1048608 | tf_op jit(solution)/shard_map/ppermute | solution.py:94
  522.2 13.7 %collective-permute-done.25 = f32[1024,256]{0,1:T(8,128)S(1)} collective-permute-done((f32[1024,256]{0,1:T(8,128)S(1)}, f32[1024,256]{0,1:T(8,128)S(1)}, u32[]{:S(2)}, u32[]{:S(2)}) %collective-permute-start.25) | collective-permute-done | bytes 1048608 | tf_op jit(solution)/shard_map/ppermute | solution.py:94
  538.2 9.2 %collective-permute-done.27 = f32[1024,256]{0,1:T(8,128)S(1)} collective-permute-done((f32[1024,256]{0,1:T(8,128)S(1)}, f32[1024,256]{0,1:T(8,128)S(1)}, u32[]{:S(2)}, u32[]{:S(2)}) %collective-permute-start.27) | collective-permute-done | bytes 1048608 | tf_op jit(solution)/shard_map/ppermute | solution.py:94
  552.3 5.3 copy.9
  557.6 17.9 %all-reduce = (f32[1024]{0:T(1024)S(1)}, f32[1024]{0:T(1024)}) all-reduce(f32[1024]{0:T(1024)S(1)} %pad_maximum_fusion.1, f32[1024]{0:T(1024)S(1)} %get-tuple-element.40), channel_id=1, replica_groups=mesh['row'=8,'col'=4] {'row'}, use_global_device_ids=true, to_apply=%region_6.7 | all-reduce | flops 2048 | bytes 16384 | tf_op jit(solution)/shard_map/psum | solution.py:125
  (141 shorter events, 145.8 us)
Async XLA Ops:
  7.2 63.4 %all-gather.2.cloned.1.call-start = ((), (), s32[]{:S(2)}) async-start(), calls=%async_computation | async-start | bytes 10485760 | tf_op jit(solution)/shard_map/all_gather | solution.py:39
  18.7 28.4 %collective-permute-start = (f32[1024,256]{0,1:T(8,128)S(1)}, f32[1024,256]{0,1:T(8,128)S(1)}, u32[]{:S(2)}, u32[]{:S(2)}) collective-permute-start(f32[1024,256]{0,1:T(8,128)S(1)} %convolution_bitcast_fusion.11), channel_id=1, source_target_pairs={{0,4},{1,5},{2,6},{3,7}} | collective-permute-start | bytes 3145736 | tf_op jit(solution)/shard_map/ppermute | solution.py:50
  28.3 65.7 %collective-permute-start.2 = (f32[1024,256]{0,1:T(8,128)}, f32[1024,256]{0,1:T(8,128)S(1)}, u32[]{:S(2)}, u32[]{:S(2)}) collective-permute-start(f32[1024,256]{0,1:T(8,128)} %convolution_bitcast_fusion.9), channel_id=1, source_target_pairs={{0,4},{1,5},{2,6},{3,7}} | collective-permute-start | bytes 3145736 | tf_op jit(solution)/shard_map/ppermute | solution.py:50
  47.2 32.6 %copy-start.14 = (f32[1024,256]{0,1:T(8,128)}, f32[1024,256]{0,1:T(8,128)S(1)}, u32[]{:S(2)}) copy-start(f32[1024,256]{0,1:T(8,128)S(1)} %collective-permute-done) | copy-start | bytes 3145732
  79.8 26.5 %collective-permute-start.1 = (f32[1024,256]{0,1:T(8,128)}, f32[1024,256]{0,1:T(8,128)}, u32[]{:S(2)}, u32[]{:S(2)}) collective-permute-start(f32[1024,256]{0,1:T(8,128)} %fusion.90), channel_id=1, source_target_pairs={{0,8},{4,12},{1,9},{5,13},{2,10},{6,14},{3,11},{7,15}} | collective-permute-start | bytes 3145736 | tf_op jit(solution)/shard_map/ppermute | solution.py:71
  90.1 32.9 %collective-permute-start.4 = (f32[1024,256]{0,1:T(8,128)}, f32[1024,256]{0,1:T(8,128)S(1)}, u32[]{:S(2)}, u32[]{:S(2)}) collective-permute-start(f32[1024,256]{0,1:T(8,128)} %convolution_bitcast_fusion.7), channel_id=1, source_target_pairs={{0,4},{1,5},{2,6},{3,7}} | collective-permute-start | bytes 3145736 | tf_op jit(solution)/shard_map/ppermute | solution.py:50
  111.2 26.7 %collective-permute-start.3 = (f32[1024,256]{0,1:T(8,128)S(1)}, f32[1024,256]{0,1:T(8,128)S(1)}, u32[]{:S(2)}, u32[]{:S(2)}) collective-permute-start(f32[1024,256]{0,1:T(8,128)S(1)} %fusion.89), channel_id=1, source_target_pairs={{0,8},{4,12},{8,16},{12,20},{1,9},{5,13},{9,17},{13,21},{2,10},{6,... | collective-permute-start | bytes 3145736 | tf_op jit(solution)/shard_map/ppermute | solution.py:71
  119.7 28.0 %collective-permute-start.6 = (f32[1024,256]{0,1:T(8,128)S(1)}, f32[1024,256]{0,1:T(8,128)S(1)}, u32[]{:S(2)}, u32[]{:S(2)}) collective-permute-start(f32[1024,256]{0,1:T(8,128)S(1)} %convolution_bitcast_fusion.5), channel_id=1, source_target_pairs={{0,4},{1,5},{2,6},{3,7}} | collective-permute-start | bytes 3145736 | tf_op jit(solution)/shard_map/ppermute | solution.py:50
  143.3 25.5 %collective-permute-start.5 = (f32[1024,256]{0,1:T(8,128)S(1)}, f32[1024,256]{0,1:T(8,128)S(1)}, u32[]{:S(2)}, u32[]{:S(2)}) collective-permute-start(f32[1024,256]{0,1:T(8,128)S(1)} %fusion.87), channel_id=1, source_target_pairs={{0,8},{4,12},{8,16},{12,20},{16,24},{20,28},{1,9},{5,13},{9,17},{1... | collective-permute-start | bytes 3145736 | tf_op jit(solution)/shard_map/ppermute | solution.py:71
  173.5 24.9 %collective-permute-start.7 = (f32[1024,256]{0,1:T(8,128)}, f32[1024,256]{0,1:T(8,128)}, u32[]{:S(2)}, u32[]{:S(2)}) collective-permute-start(f32[1024,256]{0,1:T(8,128)} %fusion.85), channel_id=1, source_target_pairs={{0,8},{4,12},{8,16},{12,20},{16,24},{20,28},{1,9},{5,13},{9,17},{1... | collective-permute-start | bytes 3145736 | tf_op jit(solution)/shard_map/ppermute | solution.py:71
  201.4 2.5 collective-permute-start.8
  203.1 21.2 %collective-permute-start.13 = (f32[1024,256]{0,1:T(8,128)}, f32[1024,256]{0,1:T(8,128)S(1)}, u32[]{:S(2)}, u32[]{:S(2)}) collective-permute-start(f32[1024,256]{0,1:T(8,128)} %get-tuple-element.55), channel_id=1, source_target_pairs={{8,12},{12,8},{16,20},{20,16},{24,28},{28,24},{9,13},{13,9},{17,21... | collective-permute-start | bytes 3145736 | tf_op jit(solution)/shard_map/ppermute | solution.py:57
  203.9 20.3 %collective-permute-start.9 = (f32[1024,256]{0,1:T(8,128)}, f32[1024,256]{0,1:T(8,128)S(1)}, u32[]{:S(2)}, u32[]{:S(2)}) collective-permute-start(f32[1024,256]{0,1:T(8,128)} %collective-permute-done.7), channel_id=1, source_target_pairs={{8,16},{12,20},{16,24},{20,28},{9,17},{13,21},{17,25},{21,29},{10,... | collective-permute-start | bytes 3145736 | tf_op jit(solution)/shard_map/ppermute | solution.py:71
  224.3 8.6 %collective-permute-start.14 = (f32[1024,256]{0,1:T(8,128)S(1)}, f32[1024,256]{0,1:T(8,128)S(1)}, u32[]{:S(2)}, u32[]{:S(2)}) collective-permute-start(f32[1024,256]{0,1:T(8,128)S(1)} %collective-permute-done.9), channel_id=1, source_target_pairs={{16,24},{20,28},{17,25},{21,29},{18,26},{22,30},{19,27},{23,31}} | collective-permute-start | bytes 3145736 | tf_op jit(solution)/shard_map/ppermute | solution.py:71
  236.0 12.6 %collective-permute-start.10 = (f32[1024,256]{0,1:T(8,128)S(1)}, f32[1024,256]{0,1:T(8,128)S(1)}, u32[]{:S(2)}, u32[]{:S(2)}) collective-permute-start(f32[1024,256]{0,1:T(8,128)S(1)} %slice_select_fusion.3), channel_id=1, source_target_pairs={{8,12},{12,8},{16,20},{20,16},{24,28},{28,24},{9,13},{13,9},{17,21... | collective-permute-start | bytes 3145736 | tf_op jit(solution)/shard_map/ppermute | solution.py:112
  239.0 9.9 %collective-permute-start.11 = (f32[1024,256]{0,1:T(8,128)S(1)}, f32[1024,256]{0,1:T(8,128)S(1)}, u32[]{:S(2)}, u32[]{:S(2)}) collective-permute-start(f32[1024,256]{0,1:T(8,128)S(1)} %get-tuple-element.18), channel_id=1, source_target_pairs={{8,12},{12,8},{16,20},{20,16},{24,28},{28,24},{9,13},{13,9},{17,21... | collective-permute-start | bytes 3145736 | tf_op jit(solution)/shard_map/ppermute | solution.py:57
  245.3 21.4 %collective-permute-start.15 = (f32[1024,256]{0,1:T(8,128)}, f32[1024,256]{0,1:T(8,128)}, u32[]{:S(2)}, u32[]{:S(2)}) collective-permute-start(f32[1024,256]{0,1:T(8,128)} %slice_select_fusion.2), channel_id=1, source_target_pairs={{8,12},{12,8},{16,20},{20,16},{24,28},{28,24},{9,13},{13,9},{17,21... | collective-permute-start | bytes 3145736 | tf_op jit(solution)/shard_map/ppermute | solution.py:112
  246.9 22.6 %collective-permute-start.16 = (f32[1024,256]{0,1:T(8,128)}, f32[1024,256]{0,1:T(8,128)}, u32[]{:S(2)}, u32[]{:S(2)}) collective-permute-start(f32[1024,256]{0,1:T(8,128)} %get-tuple-element.23), channel_id=1, source_target_pairs={{8,12},{12,8},{16,20},{20,16},{24,28},{28,24},{9,13},{13,9},{17,21... | collective-permute-start | bytes 3145736 | tf_op jit(solution)/shard_map/ppermute | solution.py:57
  248.9 17.8 %collective-permute-start.12 = (f32[1024,256]{0,1:T(8,128)S(1)}, f32[1024,256]{0,1:T(8,128)S(1)}, u32[]{:S(2)}, u32[]{:S(2)}) collective-permute-start(f32[1024,256]{0,1:T(8,128)S(1)} %select_add_fusion.14), channel_id=1, source_target_pairs={{24,16},{28,20},{25,17},{29,21},{26,18},{30,22},{27,19},{31,23}} | collective-permute-start | bytes 3145736 | tf_op jit(solution)/shard_map/ppermute | solution.py:85
  265.8 21.4 %collective-permute-start.18 = (f32[1024,256]{0,1:T(8,128)}, f32[1024,256]{0,1:T(8,128)S(1)}, u32[]{:S(2)}, u32[]{:S(2)}) collective-permute-start(f32[1024,256]{0,1:T(8,128)} %slice_select_fusion.1), channel_id=1, source_target_pairs={{8,12},{12,8},{16,20},{20,16},{24,28},{28,24},{9,13},{13,9},{17,21... | collective-permute-start | bytes 3145736 | tf_op jit(solution)/shard_map/ppermute | solution.py:112
  278.8 8.5 %collective-permute-start.17 = (f32[1024,256]{0,1:T(8,128)S(1)}, f32[1024,256]{0,1:T(8,128)S(1)}, u32[]{:S(2)}, u32[]{:S(2)}) collective-permute-start(f32[1024,256]{0,1:T(8,128)S(1)} %copy-done.18), channel_id=1, source_target_pairs={{16,8},{20,12},{24,16},{28,20},{17,9},{21,13},{25,17},{29,21},{18,... | collective-permute-start | bytes 3145736 | tf_op jit(solution)/shard_map/ppermute | solution.py:85
  286.5 3.0 collective-permute-start.21
  287.3 139.8 %copy-start.7 = (f32[1024,256]{0,1:T(8,128)}, f32[1024,256]{0,1:T(8,128)S(1)}, u32[]{:S(2)}) copy-start(f32[1024,256]{0,1:T(8,128)S(1)} %collective-permute-done.17) | copy-start | bytes 3145732
  288.2 138.9 %collective-permute-start.19 = (f32[1024,256]{0,1:T(8,128)S(1)}, f32[1024,256]{0,1:T(8,128)S(1)}, u32[]{:S(2)}, u32[]{:S(2)}) collective-permute-start(f32[1024,256]{0,1:T(8,128)S(1)} %get-tuple-element.36), channel_id=1, source_target_pairs={{8,0},{12,4},{16,8},{20,12},{24,16},{28,20},{9,1},{13,5},{17,9},{2... | collective-permute-start | bytes 3145736 | tf_op jit(solution)/shard_map/ppermute | solution.py:85
  289.5 137.6 %copy-start.17 = (f32[1024,256]{0,1:T(8,128)}, f32[1024,256]{0,1:T(8,128)S(1)}, u32[]{:S(2)}) copy-start(f32[1024,256]{0,1:T(8,128)S(1)} %collective-permute-done.21) | copy-start | bytes 3145732
  431.3 26.3 %collective-permute-start.22 = (f32[1024,256]{0,1:T(8,128)}, f32[1024,256]{0,1:T(8,128)S(1)}, u32[]{:S(2)}, u32[]{:S(2)}) collective-permute-start(f32[1024,256]{0,1:T(8,128)} %get-tuple-element.34), channel_id=1, source_target_pairs={{8,0},{12,4},{16,8},{20,12},{24,16},{28,20},{9,1},{13,5},{17,9},{2... | collective-permute-start | bytes 3145736 | tf_op jit(solution)/shard_map/ppermute | solution.py:85
  460.1 27.3 %collective-permute-start.24 = (f32[1024,256]{0,1:T(8,128)S(1)}, f32[1024,256]{0,1:T(8,128)S(1)}, u32[]{:S(2)}, u32[]{:S(2)}) collective-permute-start(f32[1024,256]{0,1:T(8,128)S(1)} %get-tuple-element.44), channel_id=1, source_target_pairs={{8,0},{12,4},{16,8},{20,12},{9,1},{13,5},{17,9},{21,13},{10,2},{14... | collective-permute-start | bytes 3145736 | tf_op jit(solution)/shard_map/ppermute | solution.py:85
  466.1 45.3 %collective-permute-start.20 = (f32[1024,256]{0,1:T(8,128)S(1)}, f32[1024,256]{0,1:T(8,128)S(1)}, u32[]{:S(2)}, u32[]{:S(2)}) collective-permute-start(f32[1024,256]{0,1:T(8,128)S(1)} %fusion.68), channel_id=1, source_target_pairs={{4,0},{5,1},{6,2},{7,3}} | collective-permute-start | bytes 3145736 | tf_op jit(solution)/shard_map/ppermute | solution.py:94
  488.3 16.7 %collective-permute-start.26 = (f32[1024,256]{0,1:T(8,128)S(1)}, f32[1024,256]{0,1:T(8,128)S(1)}, u32[]{:S(2)}, u32[]{:S(2)}) collective-permute-start(f32[1024,256]{0,1:T(8,128)S(1)} %get-tuple-element.46), channel_id=1, source_target_pairs={{8,0},{12,4},{9,1},{13,5},{10,2},{14,6},{11,3},{15,7}} | collective-permute-start | bytes 3145736 | tf_op jit(solution)/shard_map/ppermute | solution.py:85
  491.9 28.0 %collective-permute-start.23 = (f32[1024,256]{0,1:T(8,128)S(1)}, f32[1024,256]{0,1:T(8,128)S(1)}, u32[]{:S(2)}, u32[]{:S(2)}) collective-permute-start(f32[1024,256]{0,1:T(8,128)S(1)} %fusion.71), channel_id=1, source_target_pairs={{4,0},{5,1},{6,2},{7,3}} | collective-permute-start | bytes 3145736 | tf_op jit(solution)/shard_map/ppermute | solution.py:94
  498.0 37.9 %collective-permute-start.25 = (f32[1024,256]{0,1:T(8,128)S(1)}, f32[1024,256]{0,1:T(8,128)S(1)}, u32[]{:S(2)}, u32[]{:S(2)}) collective-permute-start(f32[1024,256]{0,1:T(8,128)S(1)} %fusion.74), channel_id=1, source_target_pairs={{4,0},{5,1},{6,2},{7,3}} | collective-permute-start | bytes 3145736 | tf_op jit(solution)/shard_map/ppermute | solution.py:94
  509.8 37.7 %collective-permute-start.27 = (f32[1024,256]{0,1:T(8,128)S(1)}, f32[1024,256]{0,1:T(8,128)S(1)}, u32[]{:S(2)}, u32[]{:S(2)}) collective-permute-start(f32[1024,256]{0,1:T(8,128)S(1)} %fusion.77), channel_id=1, source_target_pairs={{4,0},{5,1},{6,2},{7,3}} | collective-permute-start | bytes 3145736 | tf_op jit(solution)/shard_map/ppermute | solution.py:94
  (21 other events, 245.5 us)
Sparse Core Ops, SparseCore 0:
  9.6 60.9 all-gather.1

commit v3 on v2

--- a/solution.py
+++ b/solution.py
@@ -3,7 +3,7 @@
 from jax import lax
 from jax.sharding import PartitionSpec as P
 
-CHUNKS = 4
+CHUNKS = 8
 
 
 def product(left, right):

time: 593 us -> 553 us (0.933)
  waiting for transfers between devices: 315 us -> 166 us
  matrix products: 143 us -> 220 us
  starting transfers between devices: 56.6 us -> 97.5 us
  other arithmetic: 30 us -> 18.3 us
    ppermute x6 -> x10, waiting for transfers between devices: 186 us -> 105 us  [hop(): lax.ppermute(sent, 'row', [link for p, _ in active for link in lanes(p, p...]
    dot_general x20 -> x40, matrix products: 82.4 us -> 131 us  [product(): return jnp.dot(left, right, precision=lax.Precision.HIGH)]
    ppermute x6 -> x10, waiting for transfers between devices: 59.1 us -> 15.1 us  [local(): lax.ppermute(sent, 'row', [link for p, _ in active for link in lanes(p, p...]
    dot_general x20 -> x40, matrix products: 54.7 us -> 83.8 us  [transposed_product(): lax.dot_general(left, right, (((0,), (0,)), ((), ())), precision=lax.Prec...]
    ppermute x6 -> x10, starting transfers between devices: 21.2 us -> 41.2 us  [local(): lax.ppermute(sent, 'row', [link for p, _ in active for link in lanes(p, p...]
    ppermute x4 -> x8, waiting for transfers between devices: 29 us -> 11.2 us  [finish(): to_zero = lax.ppermute(transposed_product(first, last), 'row', [(1, 0)])]
    ppermute x4 -> x8, waiting for transfers between devices: 17.3 us -> 0.02 us  [local(): zeros.append(lax.ppermute(start, 'row', [(0, 1)]))]
    all_gather x1, waiting for transfers between devices: 23.4 us -> 34.4 us  [local(): border = lax.all_gather(factor, 'col', axis=1, tiled=True)]
  transfers between devices with their start and end apart: 29 -> 53, of which waited for: 13 -> 19; matrix products, arithmetic and copies ran while one was open for 26% -> 39% of each run, Pallas kernels for 0% -> 0%
where the time goes in v3:
time: 553 us; the launch traced here: 543 us
  matrix products  220 us (40%)
  waiting for transfers between devices  166 us (30%)
  starting transfers between devices  97.5 us (18%)
  other arithmetic  18.3 us (3%)
  blocking collectives  18 us (3%)
  between operations  16.3 us (3%)
  local copies, waits for them, and re-layouts  5.81 us (1%)
    dot_general x40, matrix products, product(): return jnp.dot(left, right, precision=lax.Precision.HIGH)  131 us
    ppermute x10, waiting for transfers between devices, hop(): lax.ppermute(sent, 'row', [link for p, _ in active for link in lanes(p, p...  105 us
    dot_general x40, matrix products, transposed_product(): lax.dot_general(left, right, (((0,), (0,)), ((), ())), precision=lax.Prec...  83.8 us
    ppermute x10, starting transfers between devices, local(): lax.ppermute(sent, 'row', [link for p, _ in active for link in lanes(p, p...  41.2 us
    all_gather x1, waiting for transfers between devices, local(): border = lax.all_gather(factor, 'col', axis=1, tiled=True)  34.4 us
    psum x1, blocking collectives, local(): explained, mean = lax.psum((squares, weighted), 'row')  18 us
    ppermute x8, starting transfers between devices, local(): zeros.append(lax.ppermute(start, 'row', [(0, 1)]))  17.8 us
    ppermute x10, waiting for transfers between devices, local(): lax.ppermute(sent, 'row', [link for p, _ in active for link in lanes(p, p...  15.1 us
  transfers between devices with their start and end apart: 53, of which 19 were waited for; matrix products, arithmetic and copies ran while one was open for 39% of the time, Pallas kernels for 0%

profile of v3, /device:TPU:0, one launch (start us, length us, event | category | flops | bytes accessed | tf_op | source)
XLA Modules:
  0.0 542.9 jit_solution(2836704546218899804)
XLA Ops:
  9.5 5.6 %multiply_exponential_fusion = f32[1024,1024]{1,0:T(8,128)S(1)} fusion(f32[1024]{0:T(1024)S(1)} %get-tuple-element.63, f32[1024]{0:T(1024)S(1)} %get-tuple-element.62, f32[1024,128]{1,0:T(8,128)} %param.6, f32[128]{0:T(128)} %param.8, f32[1024,128]{1,0:T(8,128)} %param.7), kind=kOutput, calls=%fused_computation.1 | convolution fusion | flops 1615069184 | bytes 5251584 | tf_op jit(solution)/shard_map/dot_general | solution.py:22
  17.5 4.9 collective-permute-start
  36.2 34.4 %all-gather.2.cloned.1.call-done = f32[1024,2048]{1,0:T(8,128)} async-done(((f32[1024,512]{1,0:T(8,128)}), f32[1024,2048]{1,0:T(8,128)}) %all-gather.2.cloned.1.call-update) | async-done | bytes 8388624 | tf_op jit(solution)/shard_map/all_gather | solution.py:39
  70.6 4.3 fusion.46
  81.5 4.3 convolution_bitcast_fusion.38
  89.2 4.3 fusion.44
  93.6 3.7 fusion.43
  97.3 4.0 collective-permute-start.3
  107.2 4.2 fusion.41
  112.1 4.0 fusion.40
  116.1 4.1 collective-permute-start.5
  130.0 4.2 fusion.34
  134.3 4.4 collective-permute-start.8
  143.4 4.3 fusion.38
  149.0 4.2 fusion.32
  153.2 3.5 fusion.37
  156.7 8.3 %collective-permute-start.10 = (f32[1024,128]{0,1:T(8,128)S(1)}, f32[1024,128]{0,1:T(8,128)S(1)}, u32[]{:S(2)}, u32[]{:S(2)}) collective-permute-start(f32[1024,128]{0,1:T(8,128)S(1)} %fusion.37), channel_id=1, source_target_pairs={{0,8},{4,12},{8,16},{12,20},{16,24},{20,28},{1,9},{5,13},{9,17},{1... | collective-permute-start | bytes 1572872 | tf_op jit(solution)/shard_map/ppermute | solution.py:71
  175.6 6.2 %collective-permute-start.16 = (f32[1024,128]{0,1:T(8,128)S(1)}, f32[1024,128]{0,1:T(8,128)S(1)}, u32[]{:S(2)}, u32[]{:S(2)}) collective-permute-start(f32[1024,128]{0,1:T(8,128)S(1)} %fusion.31), channel_id=1, source_target_pairs={{0,8},{4,12},{8,16},{12,20},{16,24},{20,28},{1,9},{5,13},{9,17},{1... | collective-permute-start | bytes 1572872 | tf_op jit(solution)/shard_map/ppermute | solution.py:71
  191.7 4.4 collective-permute-start.21
  206.2 5.0 collective-permute-start.27
  235.0 3.5 fusion.21
  255.4 3.6 convolution_bitcast_fusion.4
  270.5 6.0 %fusion.19 = f32[1024,128]{1,0:T(8,128)S(1)} fusion(f32[1024,2048]{1,0:T(8,128)} %all-gather.2.cloned.1.call-done, f32[1024,128]{0,1:T(8,128)S(1)} %get-tuple-element.100, f32[1024,128]{0,1:T(8,128)S(1)} %get-tuple-element.99, f32[1024,1024]{1,0:T(8,128)S(1)} %copy-done.8), kind=kOutput, calls=%fused_computation.41 | convolution fusion | flops 1611005952 | bytes 10485760 | tf_op jit(solution)/shard_map/dot_general | solution.py:10
  285.6 46.8 %collective-permute-done.24 = f32[1024,128]{0,1:T(8,128)S(1)} collective-permute-done((f32[1024,128]{0,1:T(8,128)S(1)}, f32[1024,128]{0,1:T(8,128)S(1)}, u32[]{:S(2)}, u32[]{:S(2)}) %collective-permute-start.24) | collective-permute-done | bytes 524320 | tf_op jit(solution)/shard_map/ppermute | solution.py:85
  352.5 18.8 %collective-permute-done.30 = f32[1024,128]{0,1:T(8,128)S(1)} collective-permute-done((f32[1024,128]{0,1:T(8,128)S(1)}, f32[1024,128]{0,1:T(8,128)S(1)}, u32[]{:S(2)}, u32[]{:S(2)}) %collective-permute-start.30) | collective-permute-done | bytes 524320 | tf_op jit(solution)/shard_map/ppermute | solution.py:85
  373.2 3.5 fusion.17
  387.7 4.3 collective-permute-done.35
  407.7 13.1 %collective-permute-done.40 = f32[1024,128]{0,1:T(8,128)S(1)} collective-permute-done((f32[1024,128]{0,1:T(8,128)S(1)}, f32[1024,128]{0,1:T(8,128)S(1)}, u32[]{:S(2)}, u32[]{:S(2)}) %collective-permute-start.40) | collective-permute-done | bytes 524320 | tf_op jit(solution)/shard_map/ppermute | solution.py:85
  427.0 8.9 %collective-permute-done.43 = f32[1024,128]{0,1:T(8,128)S(1)} collective-permute-done((f32[1024,128]{0,1:T(8,128)S(1)}, f32[1024,128]{0,1:T(8,128)S(1)}, u32[]{:S(2)}, u32[]{:S(2)}) %collective-permute-start.43) | collective-permute-done | bytes 524320 | tf_op jit(solution)/shard_map/ppermute | solution.py:85
  440.8 9.8 %collective-permute-done.46 = f32[1024,128]{0,1:T(8,128)S(1)} collective-permute-done((f32[1024,128]{0,1:T(8,128)S(1)}, f32[1024,128]{0,1:T(8,128)S(1)}, u32[]{:S(2)}, u32[]{:S(2)}) %collective-permute-start.46) | collective-permute-done | bytes 524320 | tf_op jit(solution)/shard_map/ppermute | solution.py:85
  509.4 5.3 copy.9
  517.3 18.0 %all-reduce = (f32[1024]{0:T(1024)S(1)}, f32[1024]{0:T(1024)}) all-reduce(f32[1024]{0:T(1024)S(1)} %constant_dynamic-update-slice_fusion.1, f32[1024]{0:T(1024)S(1)} %multiply_reduce_fusion), channel_id=1, replica_groups=mesh['row'=8,'col'=4] {'row'}, use_global_device_ids=true, to_apply=%region_10.11 | all-reduce | flops 2048 | bytes 16384 | tf_op jit(solution)/shard_map/psum | solution.py:125
  (315 shorter events, 262.6 us)
Async XLA Ops:
  7.2 63.4 %all-gather.2.cloned.1.call-start = ((), (), s32[]{:S(2)}) async-start(), calls=%async_computation | async-start | bytes 10485760 | tf_op jit(solution)/shard_map/all_gather | solution.py:39
  17.5 18.7 %collective-permute-start = (f32[1024,128]{0,1:T(8,128)S(1)}, f32[1024,128]{0,1:T(8,128)S(1)}, u32[]{:S(2)}, u32[]{:S(2)}) collective-permute-start(f32[1024,128]{0,1:T(8,128)S(1)} %convolution_bitcast_fusion.47), channel_id=1, source_target_pairs={{0,4},{1,5},{2,6},{3,7}} | collective-permute-start | bytes 1572872 | tf_op jit(solution)/shard_map/ppermute | solution.py:50
  25.6 63.6 %collective-permute-start.2 = (f32[1024,128]{0,1:T(8,128)}, f32[1024,128]{0,1:T(8,128)S(1)}, u32[]{:S(2)}, u32[]{:S(2)}) collective-permute-start(f32[1024,128]{0,1:T(8,128)} %convolution_bitcast_fusion.44), channel_id=1, source_target_pairs={{0,4},{1,5},{2,6},{3,7}} | collective-permute-start | bytes 1572872 | tf_op jit(solution)/shard_map/ppermute | solution.py:50
  30.1 77.1 %collective-permute-start.4 = (f32[1024,128]{0,1:T(8,128)}, f32[1024,128]{0,1:T(8,128)S(1)}, u32[]{:S(2)}, u32[]{:S(2)}) collective-permute-start(f32[1024,128]{0,1:T(8,128)} %convolution_bitcast_fusion.41), channel_id=1, source_target_pairs={{0,4},{1,5},{2,6},{3,7}} | collective-permute-start | bytes 1572872 | tf_op jit(solution)/shard_map/ppermute | solution.py:50
  34.6 90.1 %collective-permute-start.7 = (f32[1024,128]{0,1:T(8,128)}, f32[1024,128]{0,1:T(8,128)S(1)}, u32[]{:S(2)}, u32[]{:S(2)}) collective-permute-start(f32[1024,128]{0,1:T(8,128)} %convolution_bitcast_fusion.35), channel_id=1, source_target_pairs={{0,4},{1,5},{2,6},{3,7}} | collective-permute-start | bytes 1572872 | tf_op jit(solution)/shard_map/ppermute | solution.py:50
  78.1 15.5 %collective-permute-start.1 = (f32[1024,128]{0,1:T(8,128)}, f32[1024,128]{0,1:T(8,128)S(1)}, u32[]{:S(2)}, u32[]{:S(2)}) collective-permute-start(f32[1024,128]{0,1:T(8,128)} %fusion.45), channel_id=1, source_target_pairs={{0,8},{4,12},{1,9},{5,13},{2,10},{6,14},{3,11},{7,15}} | collective-permute-start | bytes 1572872 | tf_op jit(solution)/shard_map/ppermute | solution.py:71
  85.7 57.7 %collective-permute-start.6 = (f32[1024,128]{0,1:T(8,128)}, f32[1024,128]{0,1:T(8,128)S(1)}, u32[]{:S(2)}, u32[]{:S(2)}) collective-permute-start(f32[1024,128]{0,1:T(8,128)} %convolution_bitcast_fusion.38), channel_id=1, source_target_pairs={{0,4},{1,5},{2,6},{3,7}} | collective-permute-start | bytes 1572872 | tf_op jit(solution)/shard_map/ppermute | solution.py:50
  104.6 44.4 %collective-permute-start.14 = (f32[1024,128]{0,1:T(8,128)}, f32[1024,128]{0,1:T(8,128)S(1)}, u32[]{:S(2)}, u32[]{:S(2)}) collective-permute-start(f32[1024,128]{0,1:T(8,128)} %convolution_bitcast_fusion.32), channel_id=1, source_target_pairs={{0,4},{1,5},{2,6},{3,7}} | collective-permute-start | bytes 1572872 | tf_op jit(solution)/shard_map/ppermute | solution.py:50
  123.4 41.7 %collective-permute-start.20 = (f32[1024,128]{0,1:T(8,128)}, f32[1024,128]{0,1:T(8,128)S(1)}, u32[]{:S(2)}, u32[]{:S(2)}) collective-permute-start(f32[1024,128]{0,1:T(8,128)} %convolution_bitcast_fusion.29), channel_id=1, source_target_pairs={{0,4},{1,5},{2,6},{3,7}} | collective-permute-start | bytes 1572872 | tf_op jit(solution)/shard_map/ppermute | solution.py:50
  141.9 25.8 %collective-permute-start.26 = (f32[1024,128]{0,1:T(8,128)}, f32[1024,128]{0,1:T(8,128)S(1)}, u32[]{:S(2)}, u32[]{:S(2)}) collective-permute-start(f32[1024,128]{0,1:T(8,128)} %convolution_bitcast_fusion.25), channel_id=1, source_target_pairs={{0,4},{1,5},{2,6},{3,7}} | collective-permute-start | bytes 1572872 | tf_op jit(solution)/shard_map/ppermute | solution.py:50
  156.7 15.4 %collective-permute-start.10 = (f32[1024,128]{0,1:T(8,128)S(1)}, f32[1024,128]{0,1:T(8,128)S(1)}, u32[]{:S(2)}, u32[]{:S(2)}) collective-permute-start(f32[1024,128]{0,1:T(8,128)S(1)} %fusion.37), channel_id=1, source_target_pairs={{0,8},{4,12},{8,16},{12,20},{16,24},{20,28},{1,9},{5,13},{9,17},{1... | collective-permute-start | bytes 1572872 | tf_op jit(solution)/shard_map/ppermute | solution.py:71
  264.5 21.1 %collective-permute-start.28 = (f32[1024,128]{0,1:T(8,128)}, f32[1024,128]{0,1:T(8,128)S(1)}, u32[]{:S(2)}, u32[]{:S(2)}) collective-permute-start(f32[1024,128]{0,1:T(8,128)} %get-tuple-element.46), channel_id=1, source_target_pairs={{8,12},{12,8},{16,20},{20,16},{24,28},{28,24},{9,13},{13,9},{17,21... | collective-permute-start | bytes 1572872 | tf_op jit(solution)/shard_map/ppermute | solution.py:112
  265.4 68.7 %collective-permute-start.29 = (f32[1024,128]{0,1:T(8,128)}, f32[1024,128]{0,1:T(8,128)S(1)}, u32[]{:S(2)}, u32[]{:S(2)}) collective-permute-start(f32[1024,128]{0,1:T(8,128)} %get-tuple-element.47), channel_id=1, source_target_pairs={{8,12},{12,8},{16,20},{20,16},{24,28},{28,24},{9,13},{13,9},{17,21... | collective-permute-start | bytes 1572872 | tf_op jit(solution)/shard_map/ppermute | solution.py:57
  267.8 64.6 %collective-permute-start.24 = (f32[1024,128]{0,1:T(8,128)S(1)}, f32[1024,128]{0,1:T(8,128)S(1)}, u32[]{:S(2)}, u32[]{:S(2)}) collective-permute-start(f32[1024,128]{0,1:T(8,128)S(1)} %get-tuple-element.44), channel_id=1, source_target_pairs={{8,0},{12,4},{16,8},{20,12},{24,16},{28,20},{9,1},{13,5},{17,9},{2... | collective-permute-start | bytes 1572872 | tf_op jit(solution)/shard_map/ppermute | solution.py:85
  283.9 67.3 %collective-permute-start.33 = (f32[1024,128]{0,1:T(8,128)S(1)}, f32[1024,128]{0,1:T(8,128)S(1)}, u32[]{:S(2)}, u32[]{:S(2)}) collective-permute-start(f32[1024,128]{0,1:T(8,128)S(1)} %slice_select_fusion.3), channel_id=1, source_target_pairs={{8,12},{12,8},{16,20},{20,16},{24,28},{28,24},{9,13},{13,9},{17,21... | collective-permute-start | bytes 1572872 | tf_op jit(solution)/shard_map/ppermute | solution.py:112
  284.7 87.0 %collective-permute-start.34 = (f32[1024,128]{0,1:T(8,128)S(1)}, f32[1024,128]{0,1:T(8,128)S(1)}, u32[]{:S(2)}, u32[]{:S(2)}) collective-permute-start(f32[1024,128]{0,1:T(8,128)S(1)} %copy-done.42), channel_id=1, source_target_pairs={{8,12},{12,8},{16,20},{20,16},{24,28},{28,24},{9,13},{13,9},{17,21... | collective-permute-start | bytes 1572872 | tf_op jit(solution)/shard_map/ppermute | solution.py:57
  345.0 42.7 %collective-permute-start.38 = (f32[1024,128]{0,1:T(8,128)S(1)}, f32[1024,128]{0,1:T(8,128)S(1)}, u32[]{:S(2)}, u32[]{:S(2)}) collective-permute-start(f32[1024,128]{0,1:T(8,128)S(1)} %slice_select_fusion.2), channel_id=1, source_target_pairs={{8,12},{12,8},{16,20},{20,16},{24,28},{28,24},{9,13},{13,9},{17,21... | collective-permute-start | bytes 1572872 | tf_op jit(solution)/shard_map/ppermute | solution.py:112
  345.7 25.5 %collective-permute-start.30 = (f32[1024,128]{0,1:T(8,128)S(1)}, f32[1024,128]{0,1:T(8,128)S(1)}, u32[]{:S(2)}, u32[]{:S(2)}) collective-permute-start(f32[1024,128]{0,1:T(8,128)S(1)} %get-tuple-element.48), channel_id=1, source_target_pairs={{8,0},{12,4},{16,8},{20,12},{24,16},{28,20},{9,1},{13,5},{17,9},{2... | collective-permute-start | bytes 1572872 | tf_op jit(solution)/shard_map/ppermute | solution.py:85
  347.0 45.8 %collective-permute-start.39 = (f32[1024,128]{0,1:T(8,128)S(1)}, f32[1024,128]{0,1:T(8,128)S(1)}, u32[]{:S(2)}, u32[]{:S(2)}) collective-permute-start(f32[1024,128]{0,1:T(8,128)S(1)} %copy-done.39), channel_id=1, source_target_pairs={{8,12},{12,8},{16,20},{20,16},{24,28},{28,24},{9,13},{13,9},{17,21... | collective-permute-start | bytes 1572872 | tf_op jit(solution)/shard_map/ppermute | solution.py:57
  351.2 34.1 %collective-permute-start.25 = (f32[1024,128]{0,1:T(8,128)S(1)}, f32[1024,128]{0,1:T(8,128)S(1)}, u32[]{:S(2)}, u32[]{:S(2)}) collective-permute-start(f32[1024,128]{0,1:T(8,128)S(1)} %convolution_bitcast_fusion.26), channel_id=1, source_target_pairs={{4,0},{5,1},{6,2},{7,3}} | collective-permute-start | bytes 1572872 | tf_op jit(solution)/shard_map/ppermute | solution.py:94
  371.7 20.2 %collective-permute-start.35 = (f32[1024,128]{0,1:T(8,128)S(1)}, f32[1024,128]{0,1:T(8,128)S(1)}, u32[]{:S(2)}, u32[]{:S(2)}) collective-permute-start(f32[1024,128]{0,1:T(8,128)S(1)} %get-tuple-element.52), channel_id=1, source_target_pairs={{8,0},{12,4},{16,8},{20,12},{24,16},{28,20},{9,1},{13,5},{17,9},{2... | collective-permute-start | bytes 1572872 | tf_op jit(solution)/shard_map/ppermute | solution.py:85
  384.0 23.7 %collective-permute-start.42 = (f32[1024,128]{0,1:T(8,128)S(1)}, f32[1024,128]{0,1:T(8,128)S(1)}, u32[]{:S(2)}, u32[]{:S(2)}) collective-permute-start(f32[1024,128]{0,1:T(8,128)S(1)} %slice_select_fusion.1), channel_id=1, source_target_pairs={{8,12},{12,8},{16,20},{20,16},{24,28},{28,24},{9,13},{13,9},{17,21... | collective-permute-start | bytes 1572872 | tf_op jit(solution)/shard_map/ppermute | solution.py:112
  400.6 20.2 %collective-permute-start.40 = (f32[1024,128]{0,1:T(8,128)S(1)}, f32[1024,128]{0,1:T(8,128)S(1)}, u32[]{:S(2)}, u32[]{:S(2)}) collective-permute-start(f32[1024,128]{0,1:T(8,128)S(1)} %get-tuple-element.56), channel_id=1, source_target_pairs={{8,0},{12,4},{16,8},{20,12},{24,16},{28,20},{9,1},{13,5},{17,9},{2... | collective-permute-start | bytes 1572872 | tf_op jit(solution)/shard_map/ppermute | solution.py:85
  405.4 21.7 %collective-permute-start.45 = (f32[1024,128]{0,1:T(8,128)S(1)}, f32[1024,128]{0,1:T(8,128)S(1)}, u32[]{:S(2)}, u32[]{:S(2)}) collective-permute-start(f32[1024,128]{0,1:T(8,128)S(1)} %slice_select_fusion), channel_id=1, source_target_pairs={{8,12},{12,8},{16,20},{20,16},{24,28},{28,24},{9,13},{13,9},{17,21... | collective-permute-start | bytes 1572872 | tf_op jit(solution)/shard_map/ppermute | solution.py:112
  424.1 28.2 %collective-permute-start.31 = (f32[1024,128]{0,1:T(8,128)S(1)}, f32[1024,128]{0,1:T(8,128)S(1)}, u32[]{:S(2)}, u32[]{:S(2)}) collective-permute-start(f32[1024,128]{0,1:T(8,128)S(1)} %convolution_bitcast_fusion.22), channel_id=1, source_target_pairs={{4,0},{5,1},{6,2},{7,3}} | collective-permute-start | bytes 1572872 | tf_op jit(solution)/shard_map/ppermute | solution.py:94
  439.5 16.7 %collective-permute-start.36 = (f32[1024,128]{0,1:T(8,128)S(1)}, f32[1024,128]{0,1:T(8,128)S(1)}, u32[]{:S(2)}, u32[]{:S(2)}) collective-permute-start(f32[1024,128]{0,1:T(8,128)S(1)} %convolution_bitcast_fusion.21), channel_id=1, source_target_pairs={{4,0},{5,1},{6,2},{7,3}} | collective-permute-start | bytes 1572872 | tf_op jit(solution)/shard_map/ppermute | solution.py:94
  462.7 19.8 %collective-permute-start.50 = (f32[1024,128]{0,1:T(8,128)S(1)}, f32[1024,128]{0,1:T(8,128)S(1)}, u32[]{:S(2)}, u32[]{:S(2)}) collective-permute-start(f32[1024,128]{0,1:T(8,128)S(1)} %get-tuple-element.80), channel_id=1, source_target_pairs={{8,0},{12,4},{9,1},{13,5},{10,2},{14,6},{11,3},{15,7}} | collective-permute-start | bytes 1572872 | tf_op jit(solution)/shard_map/ppermute | solution.py:85
  467.2 20.2 %collective-permute-start.41 = (f32[1024,128]{0,1:T(8,128)S(1)}, f32[1024,128]{0,1:T(8,128)S(1)}, u32[]{:S(2)}, u32[]{:S(2)}) collective-permute-start(f32[1024,128]{0,1:T(8,128)S(1)} %convolution_bitcast_fusion.20), channel_id=1, source_target_pairs={{4,0},{5,1},{6,2},{7,3}} | collective-permute-start | bytes 1572872 | tf_op jit(solution)/shard_map/ppermute | solution.py:94
  471.7 18.1 %collective-permute-start.44 = (f32[1024,128]{0,1:T(8,128)S(1)}, f32[1024,128]{0,1:T(8,128)S(1)}, u32[]{:S(2)}, u32[]{:S(2)}) collective-permute-start(f32[1024,128]{0,1:T(8,128)S(1)} %convolution_bitcast_fusion.19), channel_id=1, source_target_pairs={{4,0},{5,1},{6,2},{7,3}} | collective-permute-start | bytes 1572872 | tf_op jit(solution)/shard_map/ppermute | solution.py:94
  476.7 18.6 %collective-permute-start.47 = (f32[1024,128]{0,1:T(8,128)S(1)}, f32[1024,128]{0,1:T(8,128)S(1)}, u32[]{:S(2)}, u32[]{:S(2)}) collective-permute-start(f32[1024,128]{0,1:T(8,128)S(1)} %convolution_bitcast_fusion.18), channel_id=1, source_target_pairs={{4,0},{5,1},{6,2},{7,3}} | collective-permute-start | bytes 1572872 | tf_op jit(solution)/shard_map/ppermute | solution.py:94
  481.2 20.0 %collective-permute-start.49 = (f32[1024,128]{0,1:T(8,128)S(1)}, f32[1024,128]{0,1:T(8,128)S(1)}, u32[]{:S(2)}, u32[]{:S(2)}) collective-permute-start(f32[1024,128]{0,1:T(8,128)S(1)} %convolution_bitcast_fusion.17), channel_id=1, source_target_pairs={{4,0},{5,1},{6,2},{7,3}} | collective-permute-start | bytes 1572872 | tf_op jit(solution)/shard_map/ppermute | solution.py:94
  485.9 21.0 %collective-permute-start.51 = (f32[1024,128]{0,1:T(8,128)S(1)}, f32[1024,128]{0,1:T(8,128)S(1)}, u32[]{:S(2)}, u32[]{:S(2)}) collective-permute-start(f32[1024,128]{0,1:T(8,128)S(1)} %convolution_bitcast_fusion.16), channel_id=1, source_target_pairs={{4,0},{5,1},{6,2},{7,3}} | collective-permute-start | bytes 1572872 | tf_op jit(solution)/shard_map/ppermute | solution.py:94
  (78 other events, 857.1 us)
Sparse Core Ops, SparseCore 0:
  9.6 60.9 all-gather.1
